TPU v7x, 256 devices: a whole 4x4x8 slice. The times are simulated.
256 devices in a mesh: lon: 8 (over z_hi, core), lat: 32 (over x, z_lo, y).
Axes of the slice: x: 4, y: 4, z: 8 (z_hi: 4, z_lo: 2; z = z_hi * 2 + z_lo), core: 2. Of those that a mesh axis runs over, the one named last changes fastest.
Arguments:
- observed: float32 [512, 512, 256], P('lon', 'lat'), may hold values from -6 to 6
- prior_draw: float32 [512, 512, 256], P('lon', 'lat'), may hold values from -6 to 6
- noise_draw: float32 [512, 512, 256], P('lon', 'lat'), may hold values from -6 to 6
- basis_lon: float32 [512, 512], replicated, may hold values from -0.25 to 0.25
- basis_lat: float32 [512, 512], replicated, may hold values from -0.25 to 0.25
- basis_time: float32 [256, 256], replicated, may hold values from -0.375 to 0.375
- eig_lon: float32 [512], replicated, may hold values from 0.2 to 5
- eig_lat: float32 [512], replicated, may hold values from 0.2 to 5
- eig_time: float32 [256], replicated, may hold values from 0.2 to 5
Outputs:
- weights: float32 [512, 512, 256], P('lon', 'lat')
- sample: float32 [512, 512, 256], P('lon', 'lat')
All inputs are finite; a program needn't handle non-finite values.
Results may differ from a plain program's by a relative error of at most 0.000068.
Values sent between devices are 32-bit elements; how exact they have to be, the bound alone decides.
No kernel may reach another device: no remote copies, remote signals or barrier semaphores. Data moves between devices by JAX's collectives and lax.ppermute only.
A program may use at most 128 MiB of HBM per device.

v0:
```python
import jax
import jax.numpy as jnp
from jax import lax
from jax.sharding import PartitionSpec as P

NOISE_VAR = 0.25
NOISE_STD = 0.5


def toward_lat(stacked):
    return lax.all_to_all(stacked, "lat", split_axis=3, concat_axis=2, tiled=True)


def leave_lat(stacked):
    return lax.all_to_all(stacked, "lat", split_axis=2, concat_axis=3, tiled=True)


def toward_lon(stacked):
    return lax.all_to_all(stacked, "lon", split_axis=3, concat_axis=1, tiled=True)


def leave_lon(stacked):
    return lax.all_to_all(stacked, "lon", split_axis=1, concat_axis=3, tiled=True)


def product(form, stacked, basis):
    return jnp.einsum(
        form, stacked, basis, precision=lax.Precision.HIGHEST, preferred_element_type=jnp.float32
    )


def lat_forward(stacked, basis_lat):
    return product("fajc,jb->fabc", stacked, basis_lat)


def lat_backward(stacked, basis_lat):
    return product("fabc,jb->fajc", stacked, basis_lat)


def lon_forward(stacked, basis_lon):
    return product("fibc,ia->fabc", stacked, basis_lon)


def lon_backward(stacked, basis_lon):
    return product("fabc,ia->fibc", stacked, basis_lon)


def rescale(stacked, draw, lon_vals, lat_vals, time_vals):
    spectrum = lon_vals[:, None, None] * lat_vals[None, :, None] * time_vals[None, None, :]
    denom = spectrum + NOISE_VAR
    weight_hat = stacked[0] / denom
    sample_hat = jnp.sqrt(spectrum) * NOISE_VAR / denom * draw + spectrum / denom * stacked[1]
    return jnp.stack([weight_hat, sample_hat])


def on_device(
    observed, prior_draw, noise_draw, basis_lon, basis_lat, basis_time, eig_lon, eig_lat, eig_time
):
    lon_count = observed.shape[0]
    lat_count = observed.shape[1]
    lon_index = lax.axis_index("lon")
    lat_index = lax.axis_index("lat")
    stacked = jnp.stack([observed, observed - NOISE_STD * noise_draw])
    stacked = product("fijk,kc->fijc", stacked, basis_time)
    stacked = leave_lat(lat_forward(toward_lat(stacked), basis_lat))
    stacked = leave_lon(lon_forward(toward_lon(stacked), basis_lon))
    lon_vals = lax.dynamic_slice_in_dim(eig_lon, lon_index * lon_count, lon_count)
    lat_vals = lax.dynamic_slice_in_dim(eig_lat, lat_index * lat_count, lat_count)
    scaled = rescale(stacked, prior_draw, lon_vals, lat_vals, eig_time)
    result = leave_lon(lon_backward(toward_lon(scaled), basis_lon))
    result = leave_lat(lat_backward(toward_lat(result), basis_lat))
    result = product("fijc,kc->fijk", result, basis_time)
    return (result[0], result[1])


def solution(mesh):
    in_specs = (
        P("lon", "lat", None),
        P("lon", "lat", None),
        P("lon", "lat", None),
        P(),
        P(),
        P(),
        P(),
        P(),
        P(),
    )
    out_specs = (P("lon", "lat", None), P("lon", "lat", None))
    return jax.shard_map(
        on_device, mesh=mesh, in_specs=in_specs, out_specs=out_specs, check_vma=False
    )
```

profile of v0, /device:TPU:1, one launch (start us, length us, event | category | flops | bytes accessed | tf_op | source)
XLA Modules:
  0.0 634.3 jit_solution(10360448579643134706)
XLA Ops:
  13.4 36.2 %all_to_all.141 = f32[32,1,16384]{2,1,0:T(1,128)} all-to-all(f32[32,1,16384]{2,1,0:T(1,128)S(1)} %reshape.60), channel_id=1, replica_groups=mesh['lon'=8,'lat'=32] {'lat'}, dimensions={0} | all-to-all | bytes 4194304 | tf_op jit(solution)/shard_map/all_to_all | solution.py:11
  50.1 7.4 %reduce = f32[32,16384]{1,0:T(8,128)S(1)} reduce(f32[32,1,16384]{2,1,0:T(1,128)} %all_to_all.141, f32[]{:T(128)} %broadcast.54), dimensions={1}, to_apply=%all_to_all.102.reduce_sub_computation | reduce | bytes 4194308 | tf_op jit(solution)/shard_map/all_to_all | solution.py:11
  60.5 6.6 %copy.59 = f32[2,64,32,16,8]{1,4,3,2,0:T(8,128)} copy(f32[2,64,32,16,8]{1,3,0,4,2:T(8,128)} %bitcast.115) | data formatting | bytes 4194304 | tf_op jit(solution)/shard_map/all_to_all | solution.py:11
  71.3 6.0 convolution_bitcast_fusion.3
  86.8 29.9 %all_to_all.142 = f32[32,1,16384]{2,1,0:T(1,128)} all-to-all(f32[32,1,16384]{2,1,0:T(1,128)S(1)} %reshape.62), channel_id=1, replica_groups=mesh['lon'=8,'lat'=32] {'lat'}, dimensions={0} | all-to-all | bytes 4194304 | tf_op jit(solution)/shard_map/all_to_all | solution.py:15
  116.7 7.4 %reduce.1 = f32[32,16384]{1,0:T(8,128)S(1)} reduce(f32[32,1,16384]{2,1,0:T(1,128)} %all_to_all.142, f32[]{:T(128)} %broadcast.54), dimensions={1}, to_apply=%all_to_all.106.reduce_sub_computation | reduce | bytes 4194308 | tf_op jit(solution)/shard_map/all_to_all | solution.py:15
  134.2 5.9 reshape.64
  140.1 59.5 %all_to_all.143 = f32[8,1,65536]{2,1,0:T(1,128)} all-to-all(f32[8,1,65536]{2,1,0:T(1,128)S(1)} %reshape.64), channel_id=1, replica_groups=mesh['lon'=8,'lat'=32] {'lon'}, dimensions={0} | all-to-all | bytes 4194304 | tf_op jit(solution)/shard_map/all_to_all | solution.py:19
  199.6 7.2 %reduce.2 = f32[8,65536]{1,0:T(8,128)S(1)} reduce(f32[8,1,65536]{2,1,0:T(1,128)} %all_to_all.143, f32[]{:T(128)} %broadcast.54), dimensions={1}, to_apply=%all_to_all.110.reduce_sub_computation | reduce | bytes 4194308 | tf_op jit(solution)/shard_map/all_to_all | solution.py:19
  210.4 6.6 %copy.66 = f32[2,8,64,16,32]{2,1,4,3,0:T(8,128)} copy(f32[2,8,64,16,32]{2,3,0,4,1:T(8,128)} %bitcast.120) | data formatting | bytes 4194304 | tf_op jit(solution)/shard_map/all_to_all | solution.py:19
  225.7 8.4 %copy.67 = f32[2,512,16,32]{3,2,0,1:T(8,128)} copy(f32[2,512,16,32]{1,3,2,0:T(8,128)} %convolution_bitcast_fusion.2) | data formatting | bytes 4194304 | tf_op jit(solution)/shard_map/fibc,ia->fabc/transpose | solution.py:27
  234.1 8.6 %reshape.66 = f32[8,1,65536]{2,1,0:T(1,128)} reshape(f32[512,2,16,32]{3,2,1,0:T(8,128)} %bitcast.106) | data formatting | bytes 4194304
  242.7 7.7 %all-to-all-start.3 = ((f32[8,1,65536]{2,1,0:T(1,128)}), f32[8,1,65536]{2,1,0:T(1,128)}, u32[]{:S(2)}, u32[]{:S(2)}) async-start(f32[8,1,65536]{2,1,0:T(1,128)} %reshape.66), calls=%async_computation.3 | async-start | bytes 4194304 | tf_op jit(solution)/shard_map/all_to_all | solution.py:23
  254.0 44.9 %all-to-all-done.3 = f32[8,1,65536]{2,1,0:T(1,128)} async-done(((f32[8,1,65536]{2,1,0:T(1,128)}), f32[8,1,65536]{2,1,0:T(1,128)}, u32[]{:S(2)}, u32[]{:S(2)}) %all-to-all-start.3) | async-done | bytes 2097184 | tf_op jit(solution)/shard_map/all_to_all | solution.py:23
  298.9 7.2 %reduce.3 = f32[8,65536]{1,0:T(8,128)S(1)} reduce(f32[8,1,65536]{2,1,0:T(1,128)} %all-to-all-done.3, f32[]{:T(128)} %broadcast.54), dimensions={1}, to_apply=%all_to_all.114.reduce_sub_computation | reduce | bytes 4194308 | tf_op jit(solution)/shard_map/all_to_all | solution.py:23
  306.1 6.0 reshape.67
  312.1 7.0 %copy.68 = f32[2,8,64,16,32]{2,4,1,3,0:T(8,128)} copy(f32[2,8,64,16,32]{4,3,0,2,1:T(8,128)} %bitcast.107) | data formatting | bytes 4194304 | tf_op jit(solution)/shard_map/all_to_all | solution.py:23
  335.4 47.9 %all_to_all.144 = f32[8,1,65536]{2,1,0:T(1,128)} all-to-all(f32[8,1,65536]{2,1,0:T(1,128)S(1)} %reshape.68), channel_id=1, replica_groups=mesh['lon'=8,'lat'=32] {'lon'}, dimensions={0} | all-to-all | bytes 4194304 | tf_op jit(solution)/shard_map/all_to_all | solution.py:19
  383.4 7.2 %reduce.4 = f32[8,65536]{1,0:T(8,128)S(1)} reduce(f32[8,1,65536]{2,1,0:T(1,128)} %all_to_all.144, f32[]{:T(128)} %broadcast.54), dimensions={1}, to_apply=%all_to_all.117.reduce_sub_computation | reduce | bytes 4194308 | tf_op jit(solution)/shard_map/all_to_all | solution.py:19
  394.2 6.6 %copy.72 = f32[2,8,64,16,32]{2,1,4,3,0:T(8,128)} copy(f32[2,8,64,16,32]{2,3,0,4,1:T(8,128)} %bitcast.122) | data formatting | bytes 4194304 | tf_op jit(solution)/shard_map/all_to_all | solution.py:19
  409.4 8.4 %copy.73 = f32[2,512,16,32]{3,2,0,1:T(8,128)} copy(f32[2,512,16,32]{1,3,2,0:T(8,128)} %convolution_bitcast_fusion.1) | data formatting | bytes 4194304 | tf_op jit(solution)/shard_map/fabc,ia->fibc/transpose | solution.py:27
  417.8 7.4 %reshape.70 = f32[8,1,65536]{2,1,0:T(1,128)S(1)} reshape(f32[512,2,16,32]{3,2,1,0:T(8,128)} %bitcast.108) | data formatting | bytes 4194304
  425.3 62.6 %all_to_all.145 = f32[8,1,65536]{2,1,0:T(1,128)} all-to-all(f32[8,1,65536]{2,1,0:T(1,128)S(1)} %reshape.70), channel_id=1, replica_groups=mesh['lon'=8,'lat'=32] {'lon'}, dimensions={0} | all-to-all | bytes 4194304 | tf_op jit(solution)/shard_map/all_to_all | solution.py:23
  487.8 7.2 %reduce.5 = f32[8,65536]{1,0:T(8,128)S(1)} reduce(f32[8,1,65536]{2,1,0:T(1,128)} %all_to_all.145, f32[]{:T(128)} %broadcast.54), dimensions={1}, to_apply=%all_to_all.121.reduce_sub_computation | reduce | bytes 4194308 | tf_op jit(solution)/shard_map/all_to_all | solution.py:23
  495.1 6.0 reshape.71
  501.0 8.7 %copy.90 = f32[2,8,64,16,32]{2,3,0,4,1:T(8,128)} copy(f32[2,8,64,16,32]{4,3,0,2,1:T(8,128)} %bitcast.109) | data formatting | bytes 4194304 | tf_op jit(solution)/shard_map/all_to_all | solution.py:23
  514.2 30.4 %all_to_all.146 = f32[32,1,16384]{2,1,0:T(1,128)} all-to-all(f32[32,1,16384]{2,1,0:T(1,128)S(1)} %reshape.72), channel_id=1, replica_groups=mesh['lon'=8,'lat'=32] {'lat'}, dimensions={0} | all-to-all | bytes 4194304 | tf_op jit(solution)/shard_map/all_to_all | solution.py:11
  544.6 7.4 %reduce.6 = f32[32,16384]{1,0:T(8,128)S(1)} reduce(f32[32,1,16384]{2,1,0:T(1,128)} %all_to_all.146, f32[]{:T(128)} %broadcast.54), dimensions={1}, to_apply=%all_to_all.125.reduce_sub_computation | reduce | bytes 4194308 | tf_op jit(solution)/shard_map/all_to_all | solution.py:11
  555.0 6.6 %copy.77 = f32[2,64,32,16,8]{1,4,3,2,0:T(8,128)} copy(f32[2,64,32,16,8]{1,3,0,4,2:T(8,128)} %bitcast.123) | data formatting | bytes 4194304 | tf_op jit(solution)/shard_map/all_to_all | solution.py:11
  565.6 6.0 convolution_bitcast_fusion
  581.0 31.1 %all_to_all.147 = f32[32,1,16384]{2,1,0:T(1,128)} all-to-all(f32[32,1,16384]{2,1,0:T(1,128)S(1)} %reshape.74), channel_id=1, replica_groups=mesh['lon'=8,'lat'=32] {'lat'}, dimensions={0} | all-to-all | bytes 4194304 | tf_op jit(solution)/shard_map/all_to_all | solution.py:15
  612.1 7.4 %reduce.7 = f32[32,16384]{1,0:T(8,128)S(1)} reduce(f32[32,1,16384]{2,1,0:T(1,128)} %all_to_all.147, f32[]{:T(128)} %broadcast.54), dimensions={1}, to_apply=%all_to_all.129.reduce_sub_computation | reduce | bytes 4194308 | tf_op jit(solution)/shard_map/all_to_all | solution.py:15
  (50 shorter events, 119.8 us)
Async XLA Ops:
  0.6 220.3 %copy-start = (f32[512,512]{1,0:T(8,128)S(1)}, f32[512,512]{1,0:T(8,128)}, u32[]{:S(2)}) copy-start(f32[512,512]{1,0:T(8,128)} %param.12) | copy-start | bytes 3145732
  0.6 1.9 copy-start.2
  0.7 2.0 copy-start.4
  242.7 7.7 %copy-start.3 = (f32[64,16,256]{2,1,0:T(8,128)S(1)}, f32[64,16,256]{2,1,0:T(8,128)}, u32[]{:S(2)}) copy-start(f32[64,16,256]{2,1,0:T(8,128)} %param.10) | copy-start | bytes 3145732
  242.7 56.2 %all-to-all-start.3 = ((f32[8,1,65536]{2,1,0:T(1,128)}), f32[8,1,65536]{2,1,0:T(1,128)}, u32[]{:S(2)}, u32[]{:S(2)}) async-start(f32[8,1,65536]{2,1,0:T(1,128)} %reshape.66), calls=%async_computation.3 | async-start | bytes 4194304 | tf_op jit(solution)/shard_map/all_to_all | solution.py:23
  319.1 2.8 copy-start.5
  321.9 1.6 copy-start.1
where the time goes:
time: 642 us; the launch traced here: 634 us
  blocking collectives  298 us (46%)
  local copies, waits for them, and re-layouts  195 us (30%)
  other arithmetic  62.4 us (10%)
  waiting for transfers between devices  44.9 us (7%)
  matrix products  25.4 us (4%)
  starting transfers between devices  7.67 us (1%)
    all_to_all x2, blocking collectives, toward_lon(): lax.all_to_all(stacked, 'lon', split_axis=3, concat_axis=1, tiled=True)  107 us
    unnamed x29, local copies, waits for them, and re-layouts  80.4 us
    all_to_all x2, blocking collectives, toward_lat(): lax.all_to_all(stacked, 'lat', split_axis=3, concat_axis=2, tiled=True)  66.6 us
    all_to_all x1, blocking collectives, leave_lon(): lax.all_to_all(stacked, 'lon', split_axis=1, concat_axis=3, tiled=True)  62.6 us
    all_to_all x2, blocking collectives, leave_lat(): lax.all_to_all(stacked, 'lat', split_axis=2, concat_axis=3, tiled=True)  61 us
    all_to_all x1, waiting for transfers between devices, leave_lon(): lax.all_to_all(stacked, 'lon', split_axis=1, concat_axis=3, tiled=True)  44.9 us
    transpose x4, local copies, waits for them, and re-layouts, product(): jnp.einsum(form, stacked, basis, precision=lax.Precision.HIGHEST, preferr...  26.6 us
    dot_general x6, matrix products, product(): jnp.einsum(form, stacked, basis, precision=lax.Precision.HIGHEST, preferr...  25.4 us
  transfers between devices with their start and end apart: 1, of which 1 were waited for; matrix products, arithmetic and copies ran while one was open for 1% of the time, Pallas kernels for 0%

commit v1 on v0

v1 whole, which is shorter than its diff:
```python
import functools

import jax
import jax.numpy as jnp
from jax import lax
from jax.experimental import pallas as pl
from jax.experimental.pallas import tpu as pltpu
from jax.sharding import PartitionSpec as P

NOISE_VAR = 0.25
NOISE_STD = 0.5
BF16 = jnp.bfloat16
F32 = jnp.float32
VMEM = pl.BlockSpec(memory_space=pltpu.VMEM)
SMEM = pl.BlockSpec(memory_space=pltpu.SMEM)
NN = (((1,), (0,)), ((), ()))
NT = (((1,), (1,)), ((), ()))
TN = (((0,), (0,)), ((), ()))
PARAMS = pltpu.CompilerParams(vmem_limit_bytes=48 * 1024 * 1024)


def halves(value):
    high = value.astype(BF16)
    low = (value - high.astype(F32)).astype(BF16)
    return high, low


def product(left, right, dims):
    dot = functools.partial(
        lax.dot_general, dimension_numbers=dims, preferred_element_type=F32
    )
    return dot(left[0], right[0]) + (dot(left[0], right[1]) + dot(left[1], right[0]))


def interleave(first, second):
    lanes = lax.broadcasted_iota(jnp.int32, first.shape, 1)
    lower = lanes < 64
    return (
        jnp.where(lower, first, pltpu.roll(second, 64, 1)),
        jnp.where(lower, pltpu.roll(first, 64, 1), second),
    )


def bases_kernel(lon_ref, lat_ref, time_ref, lon_out, lont_out, lat_out, latt_out, time_out):
    for source, plain, flipped in (
        (lon_ref, lon_out, lont_out),
        (lat_ref, lat_out, latt_out),
    ):
        high, low = halves(source[...])
        plain[0], plain[1] = high, low
        high, low = halves(source[...].T)
        flipped[0], flipped[1] = high, low
    time_out[0], time_out[1] = halves(time_ref[...])


def forward_kernel(obs0, obs1, noise0, noise1, prior0, prior1, time_ref, out_ref):
    basis = halves(time_ref[...].T)

    def step(jj, carry):
        rows = pl.ds(jj, 64, stride=16)
        obs = jnp.concatenate([obs0[rows, :], obs1[rows, :]], axis=1)
        noise = jnp.concatenate([noise0[rows, :], noise1[rows, :]], axis=1)
        field = jnp.concatenate([obs, obs - NOISE_STD * noise], axis=0)
        out_ref[pl.ds(jj, 256, stride=24), :] = product(basis, halves(field), NT)
        return carry

    lax.fori_loop(0, 16, step, 0)

    def move(jj, carry):
        for half, prior in enumerate((prior0, prior1)):
            both = jnp.concatenate(
                [prior[pl.ds(jj, 64, stride=16), :], prior[pl.ds(jj + 8, 64, stride=16), :]],
                axis=0,
            )
            out_ref[pl.ds(half * 3072 + 16 + jj, 128, stride=24), :] = both.T
        return carry

    lax.fori_loop(0, 8, move, 0)


def middle_kernel(
    in_ref, lon_ref, lont_ref, lat_ref, latt_ref, vals_lon, vals_lat, val_time, out_ref,
    x_ref, y_ref, prior_ref, scaled_ref, v_ref,
):
    for p in range(4):
        def gather(blk, carry):
            rows = pl.ds(pl.multiple_of(blk * 128, 128), 128)
            even = pl.ds(p * 64 + blk * 8, 8)
            odd = pl.ds(p * 64 + 32 + blk * 8, 8)
            pair = interleave(
                in_ref[even, 0:16, :].reshape(128, 128), in_ref[odd, 0:16, :].reshape(128, 128)
            )
            for f in range(2):
                high, low = halves(pair[f])
                x_ref[0, rows, f * 512 + p * 128:f * 512 + (p + 1) * 128] = high
                x_ref[1, rows, f * 512 + p * 128:f * 512 + (p + 1) * 128] = low
            first, second = interleave(
                in_ref[even, 16:24, :].reshape(64, 128), in_ref[odd, 16:24, :].reshape(64, 128)
            )
            both = jnp.concatenate([first.reshape(8, 8, 128), second.reshape(8, 8, 128)], axis=1)
            prior_ref[rows, p * 128:(p + 1) * 128] = both.reshape(128, 128)
            return carry

        lax.fori_loop(0, 4, gather, 0)

    def lat_forward(n, carry):
        lanes = pl.ds(pl.multiple_of(n * 256, 256), 256)
        result = product(
            (latt_ref[0], latt_ref[1]), (x_ref[0, :, lanes], x_ref[1, :, lanes]), NN
        )
        y_ref[0, :, lanes], y_ref[1, :, lanes] = halves(result)
        return carry

    lax.fori_loop(0, 4, lat_forward, 0)

    def lon_forward(n, carry):
        lanes = pl.ds(pl.multiple_of(n * 256, 256), 256)
        right = (lon_ref[0, :, lanes], lon_ref[1, :, lanes])
        spectrum = vals_lon[:, lanes] * vals_lat[...] * val_time[0]
        denom = spectrum + NOISE_VAR
        hat = product((y_ref[0, :, 0:512], y_ref[1, :, 0:512]), right, NN)
        scaled_ref[0, 0, :, lanes], scaled_ref[0, 1, :, lanes] = halves(hat / denom)
        hat = product((y_ref[0, :, 512:1024], y_ref[1, :, 512:1024]), right, NN)
        sample = (
            jnp.sqrt(spectrum) * NOISE_VAR / denom * prior_ref[:, lanes] + spectrum / denom * hat
        )
        scaled_ref[1, 0, :, lanes], scaled_ref[1, 1, :, lanes] = halves(sample)
        return carry

    lax.fori_loop(0, 2, lon_forward, 0)

    for f in range(2):
        def lon_backward(n, carry):
            lanes = pl.ds(pl.multiple_of(n * 256, 256), 256)
            result = product(
                (scaled_ref[f, 0], scaled_ref[f, 1]), (lont_ref[0, :, lanes], lont_ref[1, :, lanes]), NN
            )
            high, low = halves(result)
            for half in range(2):
                target = pl.ds(pl.multiple_of(n * 512 + half * 256 + f * 128, 128), 128)
                v_ref[0, :, target] = high[:, half * 128:(half + 1) * 128]
                v_ref[1, :, target] = low[:, half * 128:(half + 1) * 128]
            return carry

        lax.fori_loop(0, 2, lon_backward, 0)

    def lat_backward(p, carry):
        lanes = pl.ds(pl.multiple_of(p * 256, 256), 256)
        result = product((lat_ref[0], lat_ref[1]), (v_ref[0, :, lanes], v_ref[1, :, lanes]), NN)
        even, odd = interleave(result[:, :128], result[:, 128:])
        out_ref[pl.ds(p * 64, 32)] = even.reshape(32, 16, 128)
        out_ref[pl.ds(p * 64 + 32, 32)] = odd.reshape(32, 16, 128)
        return carry

    lax.fori_loop(0, 4, lat_backward, 0)


def backward_kernel(in_ref, time_ref, weights_ref, sample_ref):
    basis = (time_ref[0], time_ref[1])

    def step(jj, carry):
        right = halves(in_ref[pl.ds(jj, 256, stride=16), :])
        result = product(basis, right, NN).T
        weights_ref[pl.ds(jj, 64, stride=16), :] = result[:64]
        sample_ref[pl.ds(jj, 64, stride=16), :] = result[64:]
        return carry

    lax.fori_loop(0, 16, step, 0)


def shape(dims, kind=F32):
    return jax.ShapeDtypeStruct(dims, kind)


def cost(flops, nbytes):
    return pl.CostEstimate(flops=int(flops), bytes_accessed=int(nbytes), transcendentals=0)


def on_device(
    observed, prior_draw, noise_draw, basis_lon, basis_lat, basis_time, eig_lon, eig_lat, eig_time
):
    index = lax.axis_index("lon") * 32 + lax.axis_index("lat")
    val_time = lax.dynamic_slice_in_dim(eig_time, index, 1)
    mib = 1 << 20

    lon, lont, lat, latt, time = pl.pallas_call(
        bases_kernel,
        out_shape=[shape((2, 512, 512), BF16)] * 4 + [shape((2, 256, 256), BF16)],
        in_specs=[VMEM] * 3,
        out_specs=[VMEM] * 5,
        compiler_params=PARAMS,
        cost_estimate=cost(4 * mib, 8 * mib),
        name="bases",
    )(basis_lon, basis_lat, basis_time)

    fields = [
        field.reshape(1024, 256)
        for field in (observed, observed, noise_draw, noise_draw, prior_draw, prior_draw)
    ]
    lanes0 = pl.BlockSpec((1024, 128), lambda step: (0, 0))
    lanes1 = pl.BlockSpec((1024, 128), lambda step: (0, 1))
    packed = pl.pallas_call(
        forward_kernel,
        out_shape=shape((6144, 128)),
        grid=(1,),
        in_specs=[lanes0, lanes1] * 3 + [VMEM],
        out_specs=VMEM,
        compiler_params=PARAMS,
        cost_estimate=cost(3 * 2 * 2048 * 256 * 256, 6 * mib),
        name="time_forward",
    )(*fields, basis_time)
    packed = lax.all_to_all(packed.reshape(256, 24, 128), ("lon", "lat"), 0, 0, tiled=True)

    planes = pl.pallas_call(
        middle_kernel,
        out_shape=shape((256, 16, 128)),
        in_specs=[VMEM] * 7 + [SMEM],
        out_specs=VMEM,
        scratch_shapes=[
            pltpu.VMEM((2, 512, 1024), BF16),
            pltpu.VMEM((2, 512, 1024), BF16),
            pltpu.VMEM((512, 512), F32),
            pltpu.VMEM((2, 2, 512, 512), BF16),
            pltpu.VMEM((2, 512, 1024), BF16),
        ],
        compiler_params=PARAMS,
        cost_estimate=cost(3 * 2 * 8 * 512**3, 8 * mib),
        name="middle",
    )(packed, lon, lont, lat, latt, eig_lon.reshape(1, 512), eig_lat.reshape(512, 1), val_time)
    planes = lax.all_to_all(planes, ("lon", "lat"), 0, 0, tiled=True)

    weights, sample = pl.pallas_call(
        backward_kernel,
        out_shape=[shape((1024, 256))] * 2,
        grid=(2,),
        in_specs=[
            pl.BlockSpec((4096, 128), lambda half: (0, 0)),
            pl.BlockSpec((2, 128, 256), lambda half: (0, half, 0)),
        ],
        out_specs=[pl.BlockSpec((1024, 128), lambda half: (0, half))] * 2,
        compiler_params=PARAMS,
        cost_estimate=cost(3 * 2 * 2048 * 256 * 256, 4 * mib),
        name="time_backward",
    )(planes.reshape(4096, 128), time)
    return weights.reshape(64, 16, 256), sample.reshape(64, 16, 256)


def solution(mesh):
    block = P("lon", "lat", None)
    return jax.shard_map(
        on_device,
        mesh=mesh,
        in_specs=(block,) * 3 + (P(),) * 6,
        out_specs=(block, block),
        check_vma=False,
    )
```

time: 642 us -> 195 us (0.30); the launches traced: 634 us -> 195 us
  blocking collectives: 298 us -> 59.7 us
  local copies, waits for them, and re-layouts: 195 us -> 12 us
  other arithmetic: 62.4 us -> 0 us
  Pallas kernels: 0 us -> 37.4 us
  matrix products: 25.4 us -> 0 us
  waiting for transfers between devices: 44.9 us -> 68.2 us
  starting transfers between devices: 7.67 us -> 16.5 us
    all_to_all x7 -> x1, blocking collectives: 298 us -> 59.7 us  [on_device(): planes = lax.all_to_all(planes, ('lon', 'lat'), 0, 0, tiled=True)]
    all_to_all x15 -> x0, local copies, waits for them, and re-layouts: 73.5 us -> none  [the longest x5 21.9 us: toward_lat(): lax.all_to_all(stacked, 'lat', split_axis=3, concat_axis=2, tiled=True)]
    unnamed x29 -> x30, local copies, waits for them, and re-layouts: 80.4 us -> 11.2 us
    all_to_all x8 -> x0, other arithmetic: 58.5 us -> none  [the longest x2 14.8 us: leave_lat(): lax.all_to_all(stacked, 'lat', split_axis=2, concat_axis=3, tiled=True)]
    pallas_call x0 -> x4, Pallas kernels: none -> 37.4 us  [the longest x1 15.8 us: on_device(): pl.pallas_call(middle_kernel, out_shape=shape((256, 16, 128)), in_specs=[...]
    transpose x4 -> x0, local copies, waits for them, and re-layouts: 26.6 us -> none  [product(): jnp.einsum(form, stacked, basis, precision=lax.Precision.HIGHEST, preferr...]
    dot_general x6 -> x0, matrix products: 25.4 us -> none  [product(): jnp.einsum(form, stacked, basis, precision=lax.Precision.HIGHEST, preferr...]
    all_to_all x1, waiting for transfers between devices: 44.9 us -> 68.2 us  [on_device(): lax.all_to_all(packed.reshape(256, 24, 128), ('lon', 'lat'), 0, 0, tiled=...]
  transfers between devices with their start and end apart: 1 -> 1, of which waited for: 1 -> 1; matrix products, arithmetic and copies ran while one was open for 1% -> 0% of each run, Pallas kernels for 0% -> 1%
where the time goes in v1:
time: 195 us
  waiting for transfers between devices  68.2 us (35%)
  blocking collectives  59.7 us (31%)
  Pallas kernels  37.4 us (19%)
  starting transfers between devices  16.5 us (8%)
  local copies, waits for them, and re-layouts  12 us (6%)
    all_to_all x1, waiting for transfers between devices, on_device(): lax.all_to_all(packed.reshape(256, 24, 128), ('lon', 'lat'), 0, 0, tiled=...  68.2 us
    all_to_all x1, blocking collectives, on_device(): planes = lax.all_to_all(planes, ('lon', 'lat'), 0, 0, tiled=True)  59.7 us
    all_to_all x1, starting transfers between devices, on_device(): lax.all_to_all(packed.reshape(256, 24, 128), ('lon', 'lat'), 0, 0, tiled=...  16.5 us
    pallas_call x1, Pallas kernels, on_device(): pl.pallas_call(middle_kernel, out_shape=shape((256, 16, 128)), in_specs=[...  15.8 us
    pallas_call x1, Pallas kernels, on_device(): pl.pallas_call(backward_kernel, out_shape=[shape((1024, 256))] * 2, grid=...  11.3 us
    unnamed x30, local copies, waits for them, and re-layouts  11.2 us
    pallas_call x1, Pallas kernels, on_device(): pl.pallas_call(forward_kernel, out_shape=shape((6144, 128)), grid=(1,), i...  7.88 us
  transfers between devices with their start and end apart: 1, of which 1 were waited for; matrix products, arithmetic and copies ran while one was open for 0% of the time, Pallas kernels for 1%

profile of v1, /device:TPU:1, one launch (start us, length us, event | category | flops | bytes accessed | tf_op | source)
XLA Modules:
  0.0 194.6 jit_solution(445586379635514148)
XLA Ops:
  0.6 0.0 copy-start
  0.6 1.2 copy-done
  1.9 0.0 copy-start.1
  1.9 1.2 copy-done.1
  3.1 0.0 copy-start.2
  3.1 1.2 copy-done.2
  4.3 0.0 copy-start.3
  4.3 0.9 copy-done.3
  5.3 7.9 %time_forward.1 = f32[6144,128]{1,0:T(8,128)} custom-call(f32[1024,256]{1,0:T(8,128)S(1)} %bitcast.9, f32[1024,256]{1,0:T(8,128)S(1)} %bitcast.10, f32[1024,256]{1,0:T(8,128)S(1)} %bitcast.11, f32[1024,256]{1,0:T(8,128)S(1)} %bitcast.12, f32[1024,256]{1,0:T(8,128)S(1)} %bitcast.13, f32[1024,256]{1,0:T(8,128)S(1)} %bitcast.14, f32[256,256]{1,0:T(8,128)S(1)} %copy-done.3), custom_call_target="tpu_custom_call" | custom-call | flops 805306368 | bytes 6291456 | tf_op jit(solution)/shard_map/time_forward/pallas_call | solution.py:202
  13.1 0.0 copy-start.13
  13.1 0.0 copy-start.14
  13.1 0.0 copy-start.12
  13.2 16.5 %all-to-all-start = ((f32[256,24,128]{2,1,0:T(8,128)}), f32[256,24,128]{2,1,0:T(8,128)}, u32[]{:S(2)}, u32[]{:S(2)}) async-start(f32[256,24,128]{2,1,0:T(8,128)} %bitcast.17), calls=%async_computation | async-start | bytes 6291456 | tf_op jit(solution)/shard_map/all_to_all | solution.py:212
  29.7 0.0 copy-done.13
  29.7 0.1 copy.11.vals_lat
  29.9 0.0 copy-done.14
  29.9 0.6 dynamic_slice.3.val_time
  30.5 0.0 copy-done.4
  30.5 0.0 copy-done.5
  30.5 2.4 %bases.1 = (bf16[2,512,512]{2,1,0:T(8,128)(2,1)S(1)}, bf16[2,512,512]{2,1,0:T(8,128)(2,1)S(1)}, bf16[2,512,512]{2,1,0:T(8,128)(2,1)S(1)}, bf16[2,512,512]{2,1,0:T(8,128)(2,1)S(1)}, bf16[2,256,256]{2,1,0:T(8,128)(2,1)S(1)}) custom-call(f32[512,512]{1,0:T(8,128)S(1)} %copy-done.5, f32[512,512]{1,0:T(8,128)} %lat_ref.1, f32[256,256]{1,0:T(8,128)S(1)} %copy-done.4), custom_call_target="tpu_custom_call" | custom-call | flops 4194304 | bytes 8388608 | tf_op jit(solution)/shard_map/bases/pallas_call | solution.py:186
  32.9 0.0 copy-start.6
  32.9 1.0 copy-done.6
  33.9 1.0 copy-done.8
  34.8 1.0 copy-done.10
  35.8 68.2 %all-to-all-done.in_ref = f32[256,24,128]{2,1,0:T(8,128)} async-done(((f32[256,24,128]{2,1,0:T(8,128)}), f32[256,24,128]{2,1,0:T(8,128)}, u32[]{:S(2)}, u32[]{:S(2)}) %all-to-all-start) | async-done | bytes 3145760 | tf_op jit(solution)/shard_map/all_to_all | solution.py:212
  104.1 0.0 copy-done.12
  104.1 1.2 copy-done.7
  105.3 1.2 copy-done.9
  106.5 1.2 copy-done.11
  107.7 15.8 %middle.1 = f32[256,16,128]{2,1,0:T(8,128)} custom-call(f32[256,24,128]{2,1,0:T(8,128)} %all-to-all-done.in_ref, bf16[2,512,512]{2,1,0:T(8,128)(2,1)S(1)} %get-tuple-element.9.lon_ref, bf16[2,512,512]{2,1,0:T(8,128)(2,1)S(1)} %copy-done.7, bf16[2,512,512]{2,1,0:T(8,128)(2,1)S(1)} %copy-done.9, bf16[2,512,512]{2,1,0:T(8,128)(2,1)S(1)} %copy-done.11, ...), custom_call_target="tpu_custom_call" | custom-call | flops 6442450944 | bytes 8388608 | tf_op jit(solution)/shard_map/middle/pallas_call | solution.py:214
  123.6 59.7 %all_to_all.10 = f32[256,16,128]{2,1,0:T(8,128)S(1)} all-to-all(f32[256,16,128]{2,1,0:T(8,128)} %middle.1), channel_id=1, replica_groups=mesh['lon'=8,'lat'=32] {'lon','lat'}, dimensions={0} | all-to-all | bytes 4194304 | tf_op jit(solution)/shard_map/all_to_all | solution.py:230
  183.2 11.3 %time_backward.1 = (f32[1024,256]{1,0:T(8,128)}, f32[1024,256]{1,0:T(8,128)}) custom-call(f32[4096,128]{1,0:T(8,128)S(1)} %bitcast.15, bf16[2,256,256]{2,1,0:T(8,128)(2,1)S(1)} %get-tuple-element.13.time_ref), custom_call_target="tpu_custom_call" | custom-call | flops 805306368 | bytes 4194304 | tf_op jit(solution)/shard_map/time_backward/pallas_call | solution.py:232
  (7 shorter events, 0.0 us)
Async XLA Ops:
  0.6 1.2 copy-start
  1.9 1.2 copy-start.1
  3.1 1.2 copy-start.2
  4.3 0.9 copy-start.3
  13.1 16.6 %copy-start.13 = (f32[512]{0:T(512)S(1)}, f32[512]{0:T(512)}, u32[]{:S(2)}) copy-start(f32[512]{0:T(512)} %param.16) | copy-start | bytes 6148
  13.1 16.7 %copy-start.14 = (f32[256]{0:T(256)S(1)}, f32[256]{0:T(256)}, u32[]{:S(2)}) copy-start(f32[256]{0:T(256)} %param.17) | copy-start | bytes 3076
  13.1 17.3 %copy-start.4 = (f32[256,256]{1,0:T(8,128)S(1)}, f32[256,256]{1,0:T(8,128)}, u32[]{:S(2)}) copy-start(f32[256,256]{1,0:T(8,128)} %time_ref.3) | copy-start | bytes 786436
  13.1 17.3 %copy-start.5 = (f32[512,512]{1,0:T(8,128)S(1)}, f32[512,512]{1,0:T(8,128)}, u32[]{:S(2)}) copy-start(f32[512,512]{1,0:T(8,128)} %lon_ref.1) | copy-start | bytes 3145732
  13.1 90.9 %copy-start.12 = (f32[512]{0:T(512)S(1)}, f32[512]{0:T(512)}, u32[]{:S(2)}) copy-start(f32[512]{0:T(512)} %param.15) | copy-start | bytes 6148
  13.2 90.9 %all-to-all-start = ((f32[256,24,128]{2,1,0:T(8,128)}), f32[256,24,128]{2,1,0:T(8,128)}, u32[]{:S(2)}, u32[]{:S(2)}) async-start(f32[256,24,128]{2,1,0:T(8,128)} %bitcast.17), calls=%async_computation | async-start | bytes 6291456 | tf_op jit(solution)/shard_map/all_to_all | solution.py:212
  32.9 1.0 copy-start.6
  33.9 1.0 copy-start.8
  34.8 1.0 copy-start.10
  104.1 1.2 copy-start.7
  105.3 1.2 copy-start.9
  106.5 1.2 copy-start.11

commit v2 on v1

v2 whole, which is shorter than its diff:
```python
import functools

import jax
import jax.numpy as jnp
from jax import lax
from jax.experimental import pallas as pl
from jax.experimental.pallas import tpu as pltpu
from jax.sharding import PartitionSpec as P

NOISE_VAR = 0.25
NOISE_STD = 0.5
BF16 = jnp.bfloat16
F32 = jnp.float32
MIB = 1 << 20
VMEM = pl.BlockSpec(memory_space=pltpu.VMEM)
SMEM = pl.BlockSpec(memory_space=pltpu.SMEM)
ANY = pl.BlockSpec(memory_space=pl.ANY)
NN = (((1,), (0,)), ((), ()))
NT = (((1,), (1,)), ((), ()))


def halves(value):
    high = value.astype(BF16)
    low = (value - high.astype(F32)).astype(BF16)
    return high, low


def product(left, right, dims):
    dot = functools.partial(
        lax.dot_general, dimension_numbers=dims, preferred_element_type=F32
    )
    return dot(left[0], right[0]) + (dot(left[0], right[1]) + dot(left[1], right[0]))


def interleave(first, second):
    lanes = lax.broadcasted_iota(jnp.int32, first.shape, 1)
    lower = lanes < 64
    return (
        jnp.where(lower, first, pltpu.roll(second, 64, 1)),
        jnp.where(lower, pltpu.roll(first, 64, 1), second),
    )


def bases_kernel(lon_ref, lat_ref, vals_lon, vals_lat, val_time, bases_hbm, vals_ref, bases, sems):
    lon, lat = lon_ref[...], lat_ref[...]
    copies = []
    for index, value in enumerate((lat.T, lon, lon.T, lat)):
        bases[index, 0], bases[index, 1] = halves(value)
        copies.append(
            pltpu.make_async_copy(bases.at[index], bases_hbm.at[index], sems.at[index])
        )
        copies[-1].start()
    vals_ref[0:1, :] = vals_lon[...]
    vals_ref[1:2, :] = vals_lat[...]
    vals_ref[2:3, :] = jnp.full((1, 512), val_time[0], F32)
    vals_ref[3:8, :] = jnp.zeros((5, 512), F32)
    for copy in copies:
        copy.wait()


def forward_kernel(
    obs_hbm, noise_hbm, prior_hbm, time_hbm, out_hbm, bufs, time, field, out_ref, sems, out_sems
):
    time_copy = pltpu.make_async_copy(time_hbm, time, sems.at[12])
    time_copy.start()
    copies = {}
    for source, j_half in ((0, 0), (1, 0), (0, 1), (1, 1), (2, 0), (2, 1)):
        array = (obs_hbm, noise_hbm, prior_hbm)[source]
        for k_half in range(2):
            slot = source * 4 + j_half * 2 + k_half
            copies[slot] = pltpu.make_async_copy(
                array.at[:, pl.ds(j_half * 8, 8), pl.ds(k_half * 128, 128)],
                bufs.at[slot],
                sems.at[slot],
            )
            copies[slot].start()
    time_copy.wait()
    basis = halves(time[...].T)

    sends = []

    def send(part):
        rows = pl.ds(part * 8, 8)
        copy = pltpu.make_async_copy(
            out_ref.reshape(256, 24, 128).at[:, rows, :], out_hbm.at[:, rows, :], out_sems.at[part]
        )
        copy.start()
        sends.append(copy)

    def rows(slot, jj):
        return bufs.at[slot].reshape(512, 128)[pl.ds(jj, 64, stride=8), :]

    for j_half in range(2):
        for k_half in range(2):
            copies[j_half * 2 + k_half].wait()
            copies[4 + j_half * 2 + k_half].wait()
        for jj in range(8):
            for k_half in range(2):
                obs = rows(j_half * 2 + k_half, jj)
                shifted = obs - NOISE_STD * rows(4 + j_half * 2 + k_half, jj)
                lanes = slice(k_half * 128, (k_half + 1) * 128)
                for f, value in enumerate((obs, shifted)):
                    target = slice(jj * 128 + f * 64, jj * 128 + (f + 1) * 64)
                    high, low = halves(value)
                    field[0, target, lanes] = high
                    field[1, target, lanes] = low
        result = product(basis, (field[0], field[1]), NT)
        for jj in range(8):
            out_ref[pl.ds(j_half * 8 + jj, 256, stride=24), :] = result[:, jj * 128:(jj + 1) * 128]
        send(j_half)

    for slot in range(8, 12):
        copies[slot].wait()
    for jj in range(8):
        for k_half in range(2):
            both = jnp.concatenate([rows(8 + k_half, jj), rows(10 + k_half, jj)], axis=0)
            out_ref[pl.ds(k_half * 3072 + 16 + jj, 128, stride=24), :] = both.T
    send(2)
    for copy in sends:
        copy.wait()


def middle_kernel(
    in_ref, bases_hbm, vals_hbm, out_ref, bases, vals, x_ref, y_ref, prior_ref, sems
):
    copies = [pltpu.make_async_copy(vals_hbm, vals, sems.at[4])]
    for index in range(4):
        copies.append(pltpu.make_async_copy(bases_hbm.at[index], bases.at[index], sems.at[index]))
    for copy in copies:
        copy.start()

    for p in range(4):
        def gather(blk, carry):
            rows = pl.ds(pl.multiple_of(blk * 128, 128), 128)
            even = pl.ds(p * 64 + blk * 8, 8)
            odd = pl.ds(p * 64 + 32 + blk * 8, 8)
            pair = interleave(
                in_ref[even, 0:16, :].reshape(128, 128), in_ref[odd, 0:16, :].reshape(128, 128)
            )
            for f in range(2):
                high, low = halves(pair[f])
                x_ref[0, rows, f * 512 + p * 128:f * 512 + (p + 1) * 128] = high
                x_ref[1, rows, f * 512 + p * 128:f * 512 + (p + 1) * 128] = low
            first, second = interleave(
                in_ref[even, 16:24, :].reshape(64, 128), in_ref[odd, 16:24, :].reshape(64, 128)
            )
            both = jnp.concatenate([first.reshape(8, 8, 128), second.reshape(8, 8, 128)], axis=1)
            prior_ref[rows, p * 128:(p + 1) * 128] = both.reshape(128, 128)
            return carry

        lax.fori_loop(0, 4, gather, 0)

    for copy in copies[:2]:
        copy.wait()
    result = product((bases[0, 0], bases[0, 1]), (x_ref[0], x_ref[1]), NN)
    for f in range(2):
        rows = slice(f * 512, (f + 1) * 512)
        y_ref[0, rows, :], y_ref[1, rows, :] = halves(result[:, f * 512:(f + 1) * 512])

    copies[2].wait()
    hat = product((y_ref[0], y_ref[1]), (bases[1, 0], bases[1, 1]), NN)
    spectrum = vals[0:1, :] * jnp.broadcast_to(vals[1:2, :], (512, 512)).T * vals[2:3, :]
    inverse = 1.0 / (spectrum + NOISE_VAR)
    y_ref[0, 0:512, :], y_ref[1, 0:512, :] = halves(hat[0:512] * inverse)
    y_ref[0, 512:1024, :], y_ref[1, 512:1024, :] = halves(
        jnp.sqrt(spectrum) * NOISE_VAR * inverse * prior_ref[...] + spectrum * inverse * hat[512:1024]
    )

    copies[3].wait()
    result = product((y_ref[0], y_ref[1]), (bases[2, 0], bases[2, 1]), NN)
    for f in range(2):
        lanes = slice(f * 512, (f + 1) * 512)
        x_ref[0, :, lanes], x_ref[1, :, lanes] = halves(result[f * 512:(f + 1) * 512])

    copies[4].wait()
    result = product((bases[3, 0], bases[3, 1]), (x_ref[0], x_ref[1]), NN)
    for p in range(4):
        even, odd = interleave(
            result[:, p * 128:(p + 1) * 128], result[:, 512 + p * 128:512 + (p + 1) * 128]
        )
        out_ref[p * 64:p * 64 + 32] = even.reshape(32, 16, 128)
        out_ref[p * 64 + 32:p * 64 + 64] = odd.reshape(32, 16, 128)


def backward_kernel(in_ref, time_ref, weights_hbm, sample_hbm, field, bufs, sems):
    basis = halves(time_ref[...])
    copies = []
    for j_half in range(2):
        for jj in range(8):
            lanes = slice(jj * 128, (jj + 1) * 128)
            high, low = halves(in_ref[pl.ds(j_half * 8 + jj, 256, stride=16), :])
            field[0, :, lanes] = high
            field[1, :, lanes] = low
        for k_half in range(2):
            left = tuple(half[k_half * 128:(k_half + 1) * 128] for half in basis)
            result = product(left, (field[0], field[1]), NN)
            slots = [f * 4 + j_half * 2 + k_half for f in range(2)]
            for jj in range(8):
                block = result[:, jj * 128:(jj + 1) * 128].T
                for f in range(2):
                    target = bufs.at[slots[f]].reshape(512, 128)
                    target[pl.ds(jj, 64, stride=8), :] = block[f * 64:(f + 1) * 64]
            for f, array in enumerate((weights_hbm, sample_hbm)):
                copy = pltpu.make_async_copy(
                    bufs.at[slots[f]],
                    array.at[:, pl.ds(j_half * 8, 8), pl.ds(k_half * 128, 128)],
                    sems.at[slots[f]],
                )
                copy.start()
                copies.append(copy)
    for copy in copies:
        copy.wait()


def shape(dims, kind=F32):
    return jax.ShapeDtypeStruct(dims, kind)


def cost(flops, nbytes):
    return pl.CostEstimate(flops=int(flops), bytes_accessed=int(nbytes), transcendentals=0)


def on_device(
    observed, prior_draw, noise_draw, basis_lon, basis_lat, basis_time, eig_lon, eig_lat, eig_time
):
    index = lax.axis_index("lon") * 32 + lax.axis_index("lat")
    val_time = lax.dynamic_slice_in_dim(eig_time, index, 1)

    bases, vals = pl.pallas_call(
        bases_kernel,
        out_shape=[shape((40, 2, 512, 512), BF16), shape((8, 512))],
        in_specs=[VMEM] * 4 + [SMEM],
        out_specs=[ANY, VMEM],
        scratch_shapes=[pltpu.VMEM((4, 2, 512, 512), BF16), pltpu.SemaphoreType.DMA((4,))],
        compiler_params=pltpu.CompilerParams(vmem_limit_bytes=32 * MIB),
        cost_estimate=cost(4 * MIB, 8 * MIB),
        name="bases",
    )(basis_lon, basis_lat, eig_lon.reshape(1, 512), eig_lat.reshape(1, 512), val_time)

    packed = pl.pallas_call(
        forward_kernel,
        out_shape=shape((256, 24, 128)),
        in_specs=[ANY] * 4,
        out_specs=ANY,
        scratch_shapes=[
            pltpu.VMEM((12, 64, 8, 128), F32),
            pltpu.VMEM((256, 256), F32),
            pltpu.VMEM((2, 1024, 256), BF16),
            pltpu.VMEM((6144, 128), F32),
            pltpu.SemaphoreType.DMA((13,)),
            pltpu.SemaphoreType.DMA((3,)),
        ],
        compiler_params=pltpu.CompilerParams(vmem_limit_bytes=58 * MIB),
        cost_estimate=cost(3 * 2 * 2048 * 256 * 256, 6 * MIB),
        name="time_forward",
    )(observed, noise_draw, prior_draw, basis_time)
    packed = lax.all_to_all(packed, ("lon", "lat"), 0, 0, tiled=True)

    planes = pl.pallas_call(
        middle_kernel,
        out_shape=shape((256, 16, 128)),
        in_specs=[VMEM, ANY, ANY],
        out_specs=VMEM,
        scratch_shapes=[
            pltpu.VMEM((4, 2, 512, 512), BF16),
            pltpu.VMEM((8, 512), F32),
            pltpu.VMEM((2, 512, 1024), BF16),
            pltpu.VMEM((2, 1024, 512), BF16),
            pltpu.VMEM((512, 512), F32),
            pltpu.SemaphoreType.DMA((5,)),
        ],
        compiler_params=pltpu.CompilerParams(vmem_limit_bytes=32 * MIB),
        cost_estimate=cost(3 * 2 * 8 * 512**3, 8 * MIB),
        name="middle",
    )(packed, bases, vals)
    planes = lax.all_to_all(planes, ("lon", "lat"), 0, 0, tiled=True)

    weights, sample = pl.pallas_call(
        backward_kernel,
        out_shape=[shape((64, 16, 256))] * 2,
        in_specs=[VMEM] * 2,
        out_specs=[ANY] * 2,
        scratch_shapes=[
            pltpu.VMEM((2, 256, 1024), BF16),
            pltpu.VMEM((8, 64, 8, 128), F32),
            pltpu.SemaphoreType.DMA((8,)),
        ],
        compiler_params=pltpu.CompilerParams(vmem_limit_bytes=32 * MIB),
        cost_estimate=cost(3 * 2 * 2048 * 256 * 256, 4 * MIB),
        name="time_backward",
    )(planes.reshape(4096, 128), basis_time)
    return weights, sample


def solution(mesh):
    block = P("lon", "lat", None)
    return jax.shard_map(
        on_device,
        mesh=mesh,
        in_specs=(block,) * 3 + (P(),) * 6,
        out_specs=(block, block),
        check_vma=False,
    )
```

time: 195 us -> 169 us (0.87)
  Pallas kernels: 37.4 us -> 20.4 us
  local copies, waits for them, and re-layouts: 12 us -> 3.06 us
    pallas_call x3, Pallas kernels: 21.6 us -> 10.5 us  [the longest x1 4.57 us: on_device(): pl.pallas_call(forward_kernel, out_shape=shape((256, 24, 128)), in_specs=...]
    unnamed x30 -> x12, local copies, waits for them, and re-layouts: 11.2 us -> 2.47 us
    pallas_call x1, Pallas kernels: 15.8 us -> 9.86 us  [on_device(): pl.pallas_call(middle_kernel, out_shape=shape((256, 16, 128)), in_specs=[...]
  transfers between devices with their start and end apart: 1 -> 1, of which waited for: 1 -> 1; matrix products, arithmetic and copies ran while one was open for 0% -> 0% of each run, Pallas kernels for 1% -> 2%
where the time goes in v2:
time: 169 us; the launch traced here: 168 us
  waiting for transfers between devices  69.1 us (41%)
  blocking collectives  59.5 us (35%)
  Pallas kernels  20.4 us (12%)
  starting transfers between devices  15.7 us (9%)
  local copies, waits for them, and re-layouts  3.06 us (2%)
    all_to_all x1, waiting for transfers between devices, on_device(): packed = lax.all_to_all(packed, ('lon', 'lat'), 0, 0, tiled=True)  69.1 us
    all_to_all x1, blocking collectives, on_device(): planes = lax.all_to_all(planes, ('lon', 'lat'), 0, 0, tiled=True)  59.5 us
    all_to_all x1, starting transfers between devices, on_device(): packed = lax.all_to_all(packed, ('lon', 'lat'), 0, 0, tiled=True)  15.7 us
    pallas_call x1, Pallas kernels, on_device(): pl.pallas_call(middle_kernel, out_shape=shape((256, 16, 128)), in_specs=[...  9.86 us
    pallas_call x1, Pallas kernels, on_device(): pl.pallas_call(forward_kernel, out_shape=shape((256, 24, 128)), in_specs=...  4.57 us
  transfers between devices with their start and end apart: 1, of which 1 were waited for; matrix products, arithmetic and copies ran while one was open for 0% of the time, Pallas kernels for 2%

profile of v2, /device:TPU:1, one launch (start us, length us, event | category | flops | bytes accessed | tf_op | source)
XLA Modules:
  0.0 168.4 jit_solution(16932176061948523130)
XLA Ops:
  0.6 4.6 %time_forward.1 = f32[256,24,128]{2,1,0:T(8,128)} custom-call(f32[64,16,256]{2,1,0:T(8,128)} %obs_hbm.1, f32[64,16,256]{2,1,0:T(8,128)} %noise_hbm.1, f32[64,16,256]{2,1,0:T(8,128)} %prior_hbm.1, f32[256,256]{1,0:T(8,128)} %time_ref.1), custom_call_target="tpu_custom_call" | custom-call | flops 805306368 | bytes 6291456 | tf_op jit(solution)/shard_map/time_forward/pallas_call | solution.py:240
  5.2 0.0 copy-start.5
  5.2 0.0 copy-start.3
  5.2 0.0 copy-start.4
  5.2 15.7 %all-to-all-start = ((f32[256,24,128]{2,1,0:T(8,128)}), f32[256,24,128]{2,1,0:T(8,128)S(1)}, u32[]{:S(2)}, u32[]{:S(2)}) async-start(f32[256,24,128]{2,1,0:T(8,128)} %time_forward.1), calls=%async_computation | async-start | bytes 6291456 | tf_op jit(solution)/shard_map/all_to_all | solution.py:257
  20.9 0.0 copy-done.5
  20.9 0.6 dynamic_slice.3.val_time
  21.5 0.0 copy-done.3
  21.5 0.0 copy-done.4
  21.5 0.0 copy-start
  21.5 1.2 copy-done
  22.7 0.0 copy-start.1
  22.7 1.2 copy-done.1
  24.0 3.0 %bases.1 = (bf16[40,2,512,512]{3,2,1,0:T(8,128)(2,1)}, f32[8,512]{1,0:T(8,128)S(1)}) custom-call(f32[512,512]{1,0:T(8,128)S(1)} %copy-done, f32[512,512]{1,0:T(8,128)S(1)} %copy-done.1, f32[1,512]{1,0:T(1,128)S(1)} %bitcast.4, f32[1,512]{1,0:T(1,128)S(1)} %bitcast.5, f32[1]{0:T(128)} %dynamic_slice.3.val_time), custom_call_target="tpu_custom_call" | custom-call | flops 4194304 | bytes 8388608 | tf_op jit(solution)/shard_map/bases/pallas_call | solution.py:229
  26.9 69.1 %all-to-all-done.in_ref = f32[256,24,128]{2,1,0:T(8,128)S(1)} async-done(((f32[256,24,128]{2,1,0:T(8,128)}), f32[256,24,128]{2,1,0:T(8,128)S(1)}, u32[]{:S(2)}, u32[]{:S(2)}) %all-to-all-start) | async-done | bytes 3145760 | tf_op jit(solution)/shard_map/all_to_all | solution.py:257
  96.0 9.9 %middle.1 = f32[256,16,128]{2,1,0:T(8,128)S(1)} custom-call(f32[256,24,128]{2,1,0:T(8,128)S(1)} %all-to-all-done.in_ref, bf16[40,2,512,512]{3,2,1,0:T(8,128)(2,1)} %get-tuple-element.4.bases_hbm, f32[8,512]{1,0:T(8,128)S(1)} %get-tuple-element.5.vals_hbm), custom_call_target="tpu_custom_call" | custom-call | flops 6442450944 | bytes 8388608 | tf_op jit(solution)/shard_map/middle/pallas_call | solution.py:259
  105.9 0.0 copy-start.2
  105.9 59.5 %all_to_all.10 = f32[256,16,128]{2,1,0:T(8,128)S(1)} all-to-all(f32[256,16,128]{2,1,0:T(8,128)S(1)} %middle.1), channel_id=1, replica_groups=mesh['lon'=8,'lat'=32] {'lon','lat'}, dimensions={0} | all-to-all | bytes 4194304 | tf_op jit(solution)/shard_map/all_to_all | solution.py:276
  165.4 0.0 copy-done.2
  165.4 3.0 %time_backward.1 = (f32[64,16,256]{2,1,0:T(8,128)}, f32[64,16,256]{2,1,0:T(8,128)}) custom-call(f32[4096,128]{1,0:T(8,128)S(1)} %bitcast.3, f32[256,256]{1,0:T(8,128)S(1)} %copy-done.2), custom_call_target="tpu_custom_call" | custom-call | flops 805306368 | bytes 4194304 | tf_op jit(solution)/shard_map/time_backward/pallas_call | solution.py:278
Async XLA Ops:
  5.2 15.7 %copy-start.5 = (f32[256]{0:T(256)S(1)}, f32[256]{0:T(256)}, u32[]{:S(2)}) copy-start(f32[256]{0:T(256)} %param.17) | copy-start | bytes 3076
  5.2 16.3 %copy-start.3 = (f32[512]{0:T(512)S(1)}, f32[512]{0:T(512)}, u32[]{:S(2)}) copy-start(f32[512]{0:T(512)} %param.15) | copy-start | bytes 6148
  5.2 16.3 %copy-start.4 = (f32[512]{0:T(512)S(1)}, f32[512]{0:T(512)}, u32[]{:S(2)}) copy-start(f32[512]{0:T(512)} %param.16) | copy-start | bytes 6148
  5.2 90.8 %all-to-all-start = ((f32[256,24,128]{2,1,0:T(8,128)}), f32[256,24,128]{2,1,0:T(8,128)S(1)}, u32[]{:S(2)}, u32[]{:S(2)}) async-start(f32[256,24,128]{2,1,0:T(8,128)} %time_forward.1), calls=%async_computation | async-start | bytes 6291456 | tf_op jit(solution)/shard_map/all_to_all | solution.py:257
  21.5 1.2 copy-start
  22.7 1.2 copy-start.1
  105.9 59.5 %copy-start.2 = (f32[256,256]{1,0:T(8,128)S(1)}, f32[256,256]{1,0:T(8,128)}, u32[]{:S(2)}) copy-start(f32[256,256]{1,0:T(8,128)} %time_ref.1) | copy-start | bytes 786436

commit v3 on v2

--- a/solution.py
+++ b/solution.py
@@ -1,5 +1,3 @@
-import functools
-
 import jax
 import jax.numpy as jnp
 from jax import lax
@@ -25,11 +23,14 @@
     return high, low
 
 
-def product(left, right, dims):
-    dot = functools.partial(
-        lax.dot_general, dimension_numbers=dims, preferred_element_type=F32
+def product(left, right, dims=NN):
+    depth = dims[0][1][0]
+    return lax.dot_general(
+        jnp.concatenate([left[0], left[0], left[1]], axis=1),
+        jnp.concatenate([right[0], right[1], right[0]], axis=depth),
+        dimension_numbers=dims,
+        preferred_element_type=F32,
     )
-    return dot(left[0], right[0]) + (dot(left[0], right[1]) + dot(left[1], right[0]))
 
 
 def interleave(first, second):
@@ -41,7 +42,9 @@
     )
 
 
-def bases_kernel(lon_ref, lat_ref, vals_lon, vals_lat, val_time, bases_hbm, vals_ref, bases, sems):
+def bases_kernel(
+    lon_ref, lat_ref, vals_lon, vals_lat, val_time, bases_hbm, scales_hbm, bases, scales, sems
+):
     lon, lat = lon_ref[...], lat_ref[...]
     copies = []
     for index, value in enumerate((lat.T, lon, lon.T, lat)):
@@ -50,10 +53,14 @@
             pltpu.make_async_copy(bases.at[index], bases_hbm.at[index], sems.at[index])
         )
         copies[-1].start()
-    vals_ref[0:1, :] = vals_lon[...]
-    vals_ref[1:2, :] = vals_lat[...]
-    vals_ref[2:3, :] = jnp.full((1, 512), val_time[0], F32)
-    vals_ref[3:8, :] = jnp.zeros((5, 512), F32)
+    column = jnp.broadcast_to(vals_lat[...], (512, 512)).T
+    spectrum = vals_lon[...] * column * val_time[0]
+    inverse = 1.0 / (spectrum + NOISE_VAR)
+    scales[0] = inverse
+    scales[1] = jnp.sqrt(spectrum) * NOISE_VAR * inverse
+    scales[2] = spectrum * inverse
+    copies.append(pltpu.make_async_copy(scales, scales_hbm.at[0:3], sems.at[4]))
+    copies[-1].start()
     for copy in copies:
         copy.wait()
 
@@ -121,59 +128,59 @@
 
 
 def middle_kernel(
-    in_ref, bases_hbm, vals_hbm, out_ref, bases, vals, x_ref, y_ref, prior_ref, sems
+    in_ref, bases_hbm, scales_hbm, out_ref, bases, scales, x_ref, y_ref, prior_ref, sems
 ):
-    copies = [pltpu.make_async_copy(vals_hbm, vals, sems.at[4])]
-    for index in range(4):
-        copies.append(pltpu.make_async_copy(bases_hbm.at[index], bases.at[index], sems.at[index]))
+    copies = [
+        pltpu.make_async_copy(bases_hbm.at[index], bases.at[index], sems.at[index])
+        for index in range(4)
+    ]
+    copies.insert(2, pltpu.make_async_copy(scales_hbm.at[0:3], scales, sems.at[4]))
     for copy in copies:
         copy.start()
+    latt, lon, lont, lat = ((bases.at[index, 0], bases.at[index, 1]) for index in range(4))
+    fields = (slice(0, 512), slice(512, 1024))
+
+    def split(ref):
+        return (ref[0][...], ref[1][...])
 
     for p in range(4):
-        def gather(blk, carry):
-            rows = pl.ds(pl.multiple_of(blk * 128, 128), 128)
-            even = pl.ds(p * 64 + blk * 8, 8)
-            odd = pl.ds(p * 64 + 32 + blk * 8, 8)
+        lanes = slice(p * 128, (p + 1) * 128)
+        for block in range(4):
+            rows = slice(block * 128, (block + 1) * 128)
+            even = slice(p * 64 + block * 8, p * 64 + block * 8 + 8)
+            odd = slice(p * 64 + 32 + block * 8, p * 64 + 32 + block * 8 + 8)
             pair = interleave(
                 in_ref[even, 0:16, :].reshape(128, 128), in_ref[odd, 0:16, :].reshape(128, 128)
             )
             for f in range(2):
-                high, low = halves(pair[f])
-                x_ref[0, rows, f * 512 + p * 128:f * 512 + (p + 1) * 128] = high
-                x_ref[1, rows, f * 512 + p * 128:f * 512 + (p + 1) * 128] = low
+                target = slice(f * 512 + p * 128, f * 512 + (p + 1) * 128)
+                x_ref[0, rows, target], x_ref[1, rows, target] = halves(pair[f])
             first, second = interleave(
                 in_ref[even, 16:24, :].reshape(64, 128), in_ref[odd, 16:24, :].reshape(64, 128)
             )
             both = jnp.concatenate([first.reshape(8, 8, 128), second.reshape(8, 8, 128)], axis=1)
-            prior_ref[rows, p * 128:(p + 1) * 128] = both.reshape(128, 128)
-            return carry
-
-        lax.fori_loop(0, 4, gather, 0)
-
-    for copy in copies[:2]:
-        copy.wait()
-    result = product((bases[0, 0], bases[0, 1]), (x_ref[0], x_ref[1]), NN)
-    for f in range(2):
-        rows = slice(f * 512, (f + 1) * 512)
-        y_ref[0, rows, :], y_ref[1, rows, :] = halves(result[:, f * 512:(f + 1) * 512])
-
+            prior_ref[rows, lanes] = both.reshape(128, 128)
+
+    copies[0].wait()
+    result = product(split(latt), (x_ref[0], x_ref[1]))
+    for rows in fields:
+        y_ref[0, rows, :], y_ref[1, rows, :] = halves(result[:, rows])
+
+    copies[1].wait()
     copies[2].wait()
-    hat = product((y_ref[0], y_ref[1]), (bases[1, 0], bases[1, 1]), NN)
-    spectrum = vals[0:1, :] * jnp.broadcast_to(vals[1:2, :], (512, 512)).T * vals[2:3, :]
-    inverse = 1.0 / (spectrum + NOISE_VAR)
-    y_ref[0, 0:512, :], y_ref[1, 0:512, :] = halves(hat[0:512] * inverse)
-    y_ref[0, 512:1024, :], y_ref[1, 512:1024, :] = halves(
-        jnp.sqrt(spectrum) * NOISE_VAR * inverse * prior_ref[...] + spectrum * inverse * hat[512:1024]
-    )
+    hat = product((y_ref[0], y_ref[1]), split(lon))
+    weight_hat = hat[fields[0]] * scales[0]
+    sample_hat = scales[1] * prior_ref[...] + scales[2] * hat[fields[1]]
+    for rows, value in zip(fields, (weight_hat, sample_hat)):
+        y_ref[0, rows, :], y_ref[1, rows, :] = halves(value)
 
     copies[3].wait()
-    result = product((y_ref[0], y_ref[1]), (bases[2, 0], bases[2, 1]), NN)
-    for f in range(2):
-        lanes = slice(f * 512, (f + 1) * 512)
-        x_ref[0, :, lanes], x_ref[1, :, lanes] = halves(result[f * 512:(f + 1) * 512])
+    result = product((y_ref[0], y_ref[1]), split(lont))
+    for rows in fields:
+        x_ref[0, :, rows], x_ref[1, :, rows] = halves(result[rows])
 
     copies[4].wait()
-    result = product((bases[3, 0], bases[3, 1]), (x_ref[0], x_ref[1]), NN)
+    result = product(split(lat), (x_ref[0], x_ref[1]))
     for p in range(4):
         even, odd = interleave(
             result[:, p * 128:(p + 1) * 128], result[:, 512 + p * 128:512 + (p + 1) * 128]
@@ -193,7 +200,7 @@
             field[1, :, lanes] = low
         for k_half in range(2):
             left = tuple(half[k_half * 128:(k_half + 1) * 128] for half in basis)
-            result = product(left, (field[0], field[1]), NN)
+            result = product(left, (field[0], field[1]))
             slots = [f * 4 + j_half * 2 + k_half for f in range(2)]
             for jj in range(8):
                 block = result[:, jj * 128:(jj + 1) * 128].T
@@ -226,12 +233,16 @@
     index = lax.axis_index("lon") * 32 + lax.axis_index("lat")
     val_time = lax.dynamic_slice_in_dim(eig_time, index, 1)
 
-    bases, vals = pl.pallas_call(
+    bases, scales = pl.pallas_call(
         bases_kernel,
-        out_shape=[shape((40, 2, 512, 512), BF16), shape((8, 512))],
+        out_shape=[shape((40, 2, 512, 512), BF16), shape((40, 512, 512))],
         in_specs=[VMEM] * 4 + [SMEM],
-        out_specs=[ANY, VMEM],
-        scratch_shapes=[pltpu.VMEM((4, 2, 512, 512), BF16), pltpu.SemaphoreType.DMA((4,))],
+        out_specs=[ANY, ANY],
+        scratch_shapes=[
+            pltpu.VMEM((4, 2, 512, 512), BF16),
+            pltpu.VMEM((3, 512, 512), F32),
+            pltpu.SemaphoreType.DMA((5,)),
+        ],
         compiler_params=pltpu.CompilerParams(vmem_limit_bytes=32 * MIB),
         cost_estimate=cost(4 * MIB, 8 * MIB),
         name="bases",
@@ -263,7 +274,7 @@
         out_specs=VMEM,
         scratch_shapes=[
             pltpu.VMEM((4, 2, 512, 512), BF16),
-            pltpu.VMEM((8, 512), F32),
+            pltpu.VMEM((3, 512, 512), F32),
             pltpu.VMEM((2, 512, 1024), BF16),
             pltpu.VMEM((2, 1024, 512), BF16),
             pltpu.VMEM((512, 512), F32),
@@ -272,7 +283,7 @@
         compiler_params=pltpu.CompilerParams(vmem_limit_bytes=32 * MIB),
         cost_estimate=cost(3 * 2 * 8 * 512**3, 8 * MIB),
         name="middle",
-    )(packed, bases, vals)
+    )(packed, bases, scales)
     planes = lax.all_to_all(planes, ("lon", "lat"), 0, 0, tiled=True)
 
     weights, sample = pl.pallas_call(

time: 169 us -> 167 us (0.988)
  no operation moved by 1% of the time
where the time goes in v3:
time: 167 us
  waiting for transfers between devices  68.1 us (41%)
  blocking collectives  59.5 us (36%)
  Pallas kernels  19.9 us (12%)
  starting transfers between devices  15.7 us (9%)
  local copies, waits for them, and re-layouts  3.06 us (2%)
    all_to_all x1, waiting for transfers between devices, on_device(): packed = lax.all_to_all(packed, ('lon', 'lat'), 0, 0, tiled=True)  68.1 us
    all_to_all x1, blocking collectives, on_device(): planes = lax.all_to_all(planes, ('lon', 'lat'), 0, 0, tiled=True)  59.5 us
    all_to_all x1, starting transfers between devices, on_device(): packed = lax.all_to_all(packed, ('lon', 'lat'), 0, 0, tiled=True)  15.7 us
    pallas_call x1, Pallas kernels, on_device(): pl.pallas_call(middle_kernel, out_shape=shape((256, 16, 128)), in_specs=[...  8.74 us
    pallas_call x1, Pallas kernels, on_device(): pl.pallas_call(forward_kernel, out_shape=shape((256, 24, 128)), in_specs=...  4.37 us
    pallas_call x1, Pallas kernels, on_device(): pl.pallas_call(bases_kernel, out_shape=[shape((40, 2, 512, 512), BF16), s...  3.95 us
  transfers between devices with their start and end apart: 1, of which 1 were waited for; matrix products, arithmetic and copies ran while one was open for 0% of the time, Pallas kernels for 2%

profile of v3, /device:TPU:1, one launch (start us, length us, event | category | flops | bytes accessed | tf_op | source)
XLA Modules:
  0.0 166.9 jit_solution(3244273780122479112)
XLA Ops:
  0.6 4.4 %time_forward.1 = f32[256,24,128]{2,1,0:T(8,128)} custom-call(f32[64,16,256]{2,1,0:T(8,128)} %obs_hbm.1, f32[64,16,256]{2,1,0:T(8,128)} %noise_hbm.1, f32[64,16,256]{2,1,0:T(8,128)} %prior_hbm.1, f32[256,256]{1,0:T(8,128)} %time_ref.1), custom_call_target="tpu_custom_call" | custom-call | flops 805306368 | bytes 6291456 | tf_op jit(solution)/shard_map/time_forward/pallas_call | solution.py:251
  5.0 0.0 copy-start.5
  5.0 0.0 copy-start.3
  5.0 0.0 copy-start.4
  5.0 15.7 %all-to-all-start = ((f32[256,24,128]{2,1,0:T(8,128)}), f32[256,24,128]{2,1,0:T(8,128)S(1)}, u32[]{:S(2)}, u32[]{:S(2)}) async-start(f32[256,24,128]{2,1,0:T(8,128)} %time_forward.1), calls=%async_computation | async-start | bytes 6291456 | tf_op jit(solution)/shard_map/all_to_all | solution.py:268
  20.7 0.0 copy-done.5
  20.7 0.6 dynamic_slice.3.val_time
  21.3 0.0 copy-done.3
  21.3 0.0 copy-done.4
  21.3 0.0 copy-start
  21.3 1.2 copy-done
  22.6 0.0 copy-start.1
  22.6 1.2 copy-done.1
  23.8 4.0 %bases.1 = (bf16[40,2,512,512]{3,2,1,0:T(8,128)(2,1)}, f32[40,512,512]{2,1,0:T(8,128)}) custom-call(f32[512,512]{1,0:T(8,128)S(1)} %copy-done, f32[512,512]{1,0:T(8,128)S(1)} %copy-done.1, f32[1,512]{1,0:T(1,128)S(1)} %bitcast.4, f32[1,512]{1,0:T(1,128)S(1)} %bitcast.5, f32[1]{0:T(128)} %dynamic_slice.3.val_time), custom_call_target="tpu_custom_call" | custom-call | flops 4194304 | bytes 8388608 | tf_op jit(solution)/shard_map/bases/pallas_call | solution.py:236
  27.7 68.1 %all-to-all-done.in_ref = f32[256,24,128]{2,1,0:T(8,128)S(1)} async-done(((f32[256,24,128]{2,1,0:T(8,128)}), f32[256,24,128]{2,1,0:T(8,128)S(1)}, u32[]{:S(2)}, u32[]{:S(2)}) %all-to-all-start) | async-done | bytes 3145760 | tf_op jit(solution)/shard_map/all_to_all | solution.py:268
  95.8 8.7 %middle.1 = f32[256,16,128]{2,1,0:T(8,128)S(1)} custom-call(f32[256,24,128]{2,1,0:T(8,128)S(1)} %all-to-all-done.in_ref, bf16[40,2,512,512]{3,2,1,0:T(8,128)(2,1)} %get-tuple-element.4.bases_hbm, f32[40,512,512]{2,1,0:T(8,128)} %get-tuple-element.5.scales_hbm), custom_call_target="tpu_custom_call" | custom-call | flops 6442450944 | bytes 8388608 | tf_op jit(solution)/shard_map/middle/pallas_call | solution.py:270
  104.6 0.0 copy-start.2
  104.6 59.5 %all_to_all.10 = f32[256,16,128]{2,1,0:T(8,128)S(1)} all-to-all(f32[256,16,128]{2,1,0:T(8,128)S(1)} %middle.1), channel_id=1, replica_groups=mesh['lon'=8,'lat'=32] {'lon','lat'}, dimensions={0} | all-to-all | bytes 4194304 | tf_op jit(solution)/shard_map/all_to_all | solution.py:287
  164.1 0.0 copy-done.2
  164.1 2.9 %time_backward.1 = (f32[64,16,256]{2,1,0:T(8,128)}, f32[64,16,256]{2,1,0:T(8,128)}) custom-call(f32[4096,128]{1,0:T(8,128)S(1)} %bitcast.3, f32[256,256]{1,0:T(8,128)S(1)} %copy-done.2), custom_call_target="tpu_custom_call" | custom-call | flops 805306368 | bytes 4194304 | tf_op jit(solution)/shard_map/time_backward/pallas_call | solution.py:289
Async XLA Ops:
  5.0 15.7 %copy-start.5 = (f32[256]{0:T(256)S(1)}, f32[256]{0:T(256)}, u32[]{:S(2)}) copy-start(f32[256]{0:T(256)} %param.17) | copy-start | bytes 3076
  5.0 16.3 %copy-start.3 = (f32[512]{0:T(512)S(1)}, f32[512]{0:T(512)}, u32[]{:S(2)}) copy-start(f32[512]{0:T(512)} %param.15) | copy-start | bytes 6148
  5.0 16.3 %copy-start.4 = (f32[512]{0:T(512)S(1)}, f32[512]{0:T(512)}, u32[]{:S(2)}) copy-start(f32[512]{0:T(512)} %param.16) | copy-start | bytes 6148
  5.0 90.8 %all-to-all-start = ((f32[256,24,128]{2,1,0:T(8,128)}), f32[256,24,128]{2,1,0:T(8,128)S(1)}, u32[]{:S(2)}, u32[]{:S(2)}) async-start(f32[256,24,128]{2,1,0:T(8,128)} %time_forward.1), calls=%async_computation | async-start | bytes 6291456 | tf_op jit(solution)/shard_map/all_to_all | solution.py:268
  21.3 1.2 copy-start
  22.6 1.2 copy-start.1
  104.6 59.5 %copy-start.2 = (f32[256,256]{1,0:T(8,128)S(1)}, f32[256,256]{1,0:T(8,128)}, u32[]{:S(2)}) copy-start(f32[256,256]{1,0:T(8,128)} %time_ref.1) | copy-start | bytes 786436

commit v4 on v3

--- a/solution.py
+++ b/solution.py
@@ -40,29 +40,6 @@
         jnp.where(lower, first, pltpu.roll(second, 64, 1)),
         jnp.where(lower, pltpu.roll(first, 64, 1), second),
     )
-
-
-def bases_kernel(
-    lon_ref, lat_ref, vals_lon, vals_lat, val_time, bases_hbm, scales_hbm, bases, scales, sems
-):
-    lon, lat = lon_ref[...], lat_ref[...]
-    copies = []
-    for index, value in enumerate((lat.T, lon, lon.T, lat)):
-        bases[index, 0], bases[index, 1] = halves(value)
-        copies.append(
-            pltpu.make_async_copy(bases.at[index], bases_hbm.at[index], sems.at[index])
-        )
-        copies[-1].start()
-    column = jnp.broadcast_to(vals_lat[...], (512, 512)).T
-    spectrum = vals_lon[...] * column * val_time[0]
-    inverse = 1.0 / (spectrum + NOISE_VAR)
-    scales[0] = inverse
-    scales[1] = jnp.sqrt(spectrum) * NOISE_VAR * inverse
-    scales[2] = spectrum * inverse
-    copies.append(pltpu.make_async_copy(scales, scales_hbm.at[0:3], sems.at[4]))
-    copies[-1].start()
-    for copy in copies:
-        copy.wait()
 
 
 def forward_kernel(
@@ -128,20 +105,10 @@
 
 
 def middle_kernel(
-    in_ref, bases_hbm, scales_hbm, out_ref, bases, scales, x_ref, y_ref, prior_ref, sems
+    in_ref, lon_ref, lat_ref, vals_lon, vals_lat, vals_time, out_ref, x_ref, y_ref, prior_ref
 ):
-    copies = [
-        pltpu.make_async_copy(bases_hbm.at[index], bases.at[index], sems.at[index])
-        for index in range(4)
-    ]
-    copies.insert(2, pltpu.make_async_copy(scales_hbm.at[0:3], scales, sems.at[4]))
-    for copy in copies:
-        copy.start()
-    latt, lon, lont, lat = ((bases.at[index, 0], bases.at[index, 1]) for index in range(4))
+    latt = halves(lat_ref[...].T)
     fields = (slice(0, 512), slice(512, 1024))
-
-    def split(ref):
-        return (ref[0][...], ref[1][...])
 
     for p in range(4):
         lanes = slice(p * 128, (p + 1) * 128)
@@ -161,26 +128,27 @@
             both = jnp.concatenate([first.reshape(8, 8, 128), second.reshape(8, 8, 128)], axis=1)
             prior_ref[rows, lanes] = both.reshape(128, 128)
 
-    copies[0].wait()
-    result = product(split(latt), (x_ref[0], x_ref[1]))
+    result = product(latt, (x_ref[0], x_ref[1]))
     for rows in fields:
         y_ref[0, rows, :], y_ref[1, rows, :] = halves(result[:, rows])
 
-    copies[1].wait()
-    copies[2].wait()
-    hat = product((y_ref[0], y_ref[1]), split(lon))
-    weight_hat = hat[fields[0]] * scales[0]
-    sample_hat = scales[1] * prior_ref[...] + scales[2] * hat[fields[1]]
+    lon = halves(lon_ref[...])
+    hat = product((y_ref[0], y_ref[1]), lon)
+    index = lax.axis_index("lon") * 32 + lax.axis_index("lat")
+    column = jnp.broadcast_to(vals_lat[...], (512, 512)).T
+    spectrum = vals_lon[...] * column * vals_time[index]
+    inverse = 1.0 / (spectrum + NOISE_VAR)
+    weight_hat = hat[fields[0]] * inverse
+    prior_scale = jnp.sqrt(spectrum) * NOISE_VAR * inverse
+    sample_hat = prior_scale * prior_ref[...] + spectrum * inverse * hat[fields[1]]
     for rows, value in zip(fields, (weight_hat, sample_hat)):
         y_ref[0, rows, :], y_ref[1, rows, :] = halves(value)
 
-    copies[3].wait()
-    result = product((y_ref[0], y_ref[1]), split(lont))
+    result = product((y_ref[0], y_ref[1]), lon, NT)
     for rows in fields:
         x_ref[0, :, rows], x_ref[1, :, rows] = halves(result[rows])
 
-    copies[4].wait()
-    result = product(split(lat), (x_ref[0], x_ref[1]))
+    result = product(halves(lat_ref[...]), (x_ref[0], x_ref[1]))
     for p in range(4):
         even, odd = interleave(
             result[:, p * 128:(p + 1) * 128], result[:, 512 + p * 128:512 + (p + 1) * 128]
@@ -230,24 +198,6 @@
 def on_device(
     observed, prior_draw, noise_draw, basis_lon, basis_lat, basis_time, eig_lon, eig_lat, eig_time
 ):
-    index = lax.axis_index("lon") * 32 + lax.axis_index("lat")
-    val_time = lax.dynamic_slice_in_dim(eig_time, index, 1)
-
-    bases, scales = pl.pallas_call(
-        bases_kernel,
-        out_shape=[shape((40, 2, 512, 512), BF16), shape((40, 512, 512))],
-        in_specs=[VMEM] * 4 + [SMEM],
-        out_specs=[ANY, ANY],
-        scratch_shapes=[
-            pltpu.VMEM((4, 2, 512, 512), BF16),
-            pltpu.VMEM((3, 512, 512), F32),
-            pltpu.SemaphoreType.DMA((5,)),
-        ],
-        compiler_params=pltpu.CompilerParams(vmem_limit_bytes=32 * MIB),
-        cost_estimate=cost(4 * MIB, 8 * MIB),
-        name="bases",
-    )(basis_lon, basis_lat, eig_lon.reshape(1, 512), eig_lat.reshape(1, 512), val_time)
-
     packed = pl.pallas_call(
         forward_kernel,
         out_shape=shape((256, 24, 128)),
@@ -270,20 +220,24 @@
     planes = pl.pallas_call(
         middle_kernel,
         out_shape=shape((256, 16, 128)),
-        in_specs=[VMEM, ANY, ANY],
+        in_specs=[VMEM] * 5 + [SMEM],
         out_specs=VMEM,
         scratch_shapes=[
-            pltpu.VMEM((4, 2, 512, 512), BF16),
-            pltpu.VMEM((3, 512, 512), F32),
             pltpu.VMEM((2, 512, 1024), BF16),
             pltpu.VMEM((2, 1024, 512), BF16),
             pltpu.VMEM((512, 512), F32),
-            pltpu.SemaphoreType.DMA((5,)),
         ],
         compiler_params=pltpu.CompilerParams(vmem_limit_bytes=32 * MIB),
         cost_estimate=cost(3 * 2 * 8 * 512**3, 8 * MIB),
         name="middle",
-    )(packed, bases, scales)
+    )(
+        packed,
+        basis_lon,
+        basis_lat,
+        eig_lon.reshape(1, 512),
+        eig_lat.reshape(1, 512),
+        eig_time,
+    )
     planes = lax.all_to_all(planes, ("lon", "lat"), 0, 0, tiled=True)
 
     weights, sample = pl.pallas_call(

time: 167 us -> 167 us (level)
  blocking collectives: 59.5 us -> 150 us
  waiting for transfers between devices: 68.1 us -> 0 us
  starting transfers between devices: 15.7 us -> 0 us
  Pallas kernels: 19.9 us -> 15.5 us
  local copies, waits for them, and re-layouts: 3.06 us -> 0.04 us
    all_to_all x0 -> x1, blocking collectives: none -> 90.8 us  [on_device(): packed = lax.all_to_all(packed, ('lon', 'lat'), 0, 0, tiled=True)]
    all_to_all x1 -> x0, waiting for transfers between devices: 68.1 us -> none  [on_device(): packed = lax.all_to_all(packed, ('lon', 'lat'), 0, 0, tiled=True)]
    all_to_all x1 -> x0, starting transfers between devices: 15.7 us -> none  [on_device(): packed = lax.all_to_all(packed, ('lon', 'lat'), 0, 0, tiled=True)]
    pallas_call x1 -> x0, Pallas kernels: 3.95 us -> none  [on_device(): pl.pallas_call(bases_kernel, out_shape=[shape((40, 2, 512, 512), BF16), s...]
    unnamed x12, local copies, waits for them, and re-layouts: 2.47 us -> 0.04 us
  transfers between devices with their start and end apart: 1 -> 0, of which waited for: 1 -> 0; matrix products, arithmetic and copies ran while one was open for 0% -> 0% of each run, Pallas kernels for 2% -> 0%
where the time goes in v4:
time: 167 us; the launch traced here: 166 us
  blocking collectives  150 us (90%)
  Pallas kernels  15.5 us (9%)
    all_to_all x1, blocking collectives, on_device(): packed = lax.all_to_all(packed, ('lon', 'lat'), 0, 0, tiled=True)  90.8 us
    all_to_all x1, blocking collectives, on_device(): planes = lax.all_to_all(planes, ('lon', 'lat'), 0, 0, tiled=True)  59.5 us
    pallas_call x1, Pallas kernels, on_device(): pl.pallas_call(middle_kernel, out_shape=shape((256, 16, 128)), in_specs=[...  8.17 us
    pallas_call x1, Pallas kernels, on_device(): pl.pallas_call(forward_kernel, out_shape=shape((256, 24, 128)), in_specs=...  4.43 us

profile of v4, /device:TPU:1, one launch (start us, length us, event | category | flops | bytes accessed | tf_op | source)
XLA Modules:
  0.0 166.5 jit_solution(7831920873154525777)
XLA Ops:
  0.6 4.4 %time_forward.1 = f32[256,24,128]{2,1,0:T(8,128)} custom-call(f32[64,16,256]{2,1,0:T(8,128)} %obs_hbm.1, f32[64,16,256]{2,1,0:T(8,128)} %noise_hbm.1, f32[64,16,256]{2,1,0:T(8,128)} %prior_hbm.1, f32[256,256]{1,0:T(8,128)} %time_ref.1), custom_call_target="tpu_custom_call" | custom-call | flops 805306368 | bytes 6291456 | tf_op jit(solution)/shard_map/time_forward/pallas_call | solution.py:201
  5.1 0.0 copy-start.1
  5.1 0.0 copy-start.2
  5.1 0.0 copy-start.3
  5.1 0.0 copy-start.4
  5.1 0.0 copy-start.5
  5.1 90.8 %all_to_all.10.in_ref = f32[256,24,128]{2,1,0:T(8,128)S(1)} all-to-all(f32[256,24,128]{2,1,0:T(8,128)} %time_forward.1), channel_id=1, replica_groups=mesh['lon'=8,'lat'=32] {'lon','lat'}, dimensions={0} | all-to-all | bytes 6291456 | tf_op jit(solution)/shard_map/all_to_all | solution.py:218
  95.9 0.0 copy-done.1
  95.9 0.0 copy-done.2
  95.9 0.0 copy-done.3
  95.9 0.0 copy-done.4
  95.9 0.0 copy-done.5
  95.9 8.2 %middle.1 = f32[256,16,128]{2,1,0:T(8,128)S(1)} custom-call(f32[256,24,128]{2,1,0:T(8,128)S(1)} %all_to_all.10.in_ref, f32[512,512]{1,0:T(8,128)S(1)} %copy-done.1, f32[512,512]{1,0:T(8,128)S(1)} %copy-done.2, f32[1,512]{1,0:T(1,128)S(1)} %bitcast.4, f32[1,512]{1,0:T(1,128)S(1)} %bitcast.5, f32[256]{0:T(256)S(1)} %copy-done.5), custom_call_target="tpu_custom_call" | custom-call | flops 6442450944 | bytes 8388608 | tf_op jit(solution)/shard_map/middle/pallas_call | solution.py:220
  104.1 0.0 copy-start
  104.1 59.5 %all_to_all.11 = f32[256,16,128]{2,1,0:T(8,128)S(1)} all-to-all(f32[256,16,128]{2,1,0:T(8,128)S(1)} %middle.1), channel_id=1, replica_groups=mesh['lon'=8,'lat'=32] {'lon','lat'}, dimensions={0} | all-to-all | bytes 4194304 | tf_op jit(solution)/shard_map/all_to_all | solution.py:241
  163.6 0.0 copy-done
  163.6 2.9 %time_backward.1 = (f32[64,16,256]{2,1,0:T(8,128)}, f32[64,16,256]{2,1,0:T(8,128)}) custom-call(f32[4096,128]{1,0:T(8,128)S(1)} %bitcast.3, f32[256,256]{1,0:T(8,128)S(1)} %copy-done), custom_call_target="tpu_custom_call" | custom-call | flops 805306368 | bytes 4194304 | tf_op jit(solution)/shard_map/time_backward/pallas_call | solution.py:243
Async XLA Ops:
  5.1 90.8 %copy-start.1 = (f32[512,512]{1,0:T(8,128)S(1)}, f32[512,512]{1,0:T(8,128)}, u32[]{:S(2)}) copy-start(f32[512,512]{1,0:T(8,128)} %lon_ref.1) | copy-start | bytes 3145732
  5.1 90.8 %copy-start.2 = (f32[512,512]{1,0:T(8,128)S(1)}, f32[512,512]{1,0:T(8,128)}, u32[]{:S(2)}) copy-start(f32[512,512]{1,0:T(8,128)} %lat_ref.1) | copy-start | bytes 3145732
  5.1 90.8 %copy-start.3 = (f32[512]{0:T(512)S(1)}, f32[512]{0:T(512)}, u32[]{:S(2)}) copy-start(f32[512]{0:T(512)} %param.15) | copy-start | bytes 6148
  5.1 90.8 %copy-start.4 = (f32[512]{0:T(512)S(1)}, f32[512]{0:T(512)}, u32[]{:S(2)}) copy-start(f32[512]{0:T(512)} %param.16) | copy-start | bytes 6148
  5.1 90.8 %copy-start.5 = (f32[256]{0:T(256)S(1)}, f32[256]{0:T(256)}, u32[]{:S(2)}) copy-start(f32[256]{0:T(256)} %vals_time.1) | copy-start | bytes 3076
  104.1 59.5 %copy-start = (f32[256,256]{1,0:T(8,128)S(1)}, f32[256,256]{1,0:T(8,128)}, u32[]{:S(2)}) copy-start(f32[256,256]{1,0:T(8,128)} %time_ref.1) | copy-start | bytes 786436

commit v5 on v4

--- a/solution.py
+++ b/solution.py
@@ -63,10 +63,12 @@
 
     sends = []
 
-    def send(part):
-        rows = pl.ds(part * 8, 8)
+    def send(part, first=0, count=256, sem=None):
+        steps, rows = pl.ds(first, count), pl.ds(part * 8, 8)
         copy = pltpu.make_async_copy(
-            out_ref.reshape(256, 24, 128).at[:, rows, :], out_hbm.at[:, rows, :], out_sems.at[part]
+            out_ref.reshape(256, 24, 128).at[steps, rows, :],
+            out_hbm.at[steps, rows, :],
+            out_sems.at[part if sem is None else sem],
         )
         copy.start()
         sends.append(copy)
@@ -95,11 +97,11 @@
 
     for slot in range(8, 12):
         copies[slot].wait()
-    for jj in range(8):
-        for k_half in range(2):
+    for k_half in range(2):
+        for jj in range(8):
             both = jnp.concatenate([rows(8 + k_half, jj), rows(10 + k_half, jj)], axis=0)
             out_ref[pl.ds(k_half * 3072 + 16 + jj, 128, stride=24), :] = both.T
-    send(2)
+        send(2, k_half * 128, 128, 2 + k_half)
     for copy in sends:
         copy.wait()
 
@@ -209,7 +211,7 @@
             pltpu.VMEM((2, 1024, 256), BF16),
             pltpu.VMEM((6144, 128), F32),
             pltpu.SemaphoreType.DMA((13,)),
-            pltpu.SemaphoreType.DMA((3,)),
+            pltpu.SemaphoreType.DMA((4,)),
         ],
         compiler_params=pltpu.CompilerParams(vmem_limit_bytes=58 * MIB),
         cost_estimate=cost(3 * 2 * 2048 * 256 * 256, 6 * MIB),

time: 167 us -> 167 us (level)
  no operation moved by 1% of the time
where the time goes in v5:
time: 167 us; the launch traced here: 166 us
  blocking collectives  150 us (90%)
  Pallas kernels  15.5 us (9%)
    all_to_all x1, blocking collectives, on_device(): packed = lax.all_to_all(packed, ('lon', 'lat'), 0, 0, tiled=True)  90.8 us
    all_to_all x1, blocking collectives, on_device(): planes = lax.all_to_all(planes, ('lon', 'lat'), 0, 0, tiled=True)  59.5 us
    pallas_call x1, Pallas kernels, on_device(): pl.pallas_call(middle_kernel, out_shape=shape((256, 16, 128)), in_specs=[...  8.18 us
    pallas_call x1, Pallas kernels, on_device(): pl.pallas_call(forward_kernel, out_shape=shape((256, 24, 128)), in_specs=...  4.44 us

profile of v5, /device:TPU:1, one launch (start us, length us, event | category | flops | bytes accessed | tf_op | source)
XLA Modules:
  0.0 166.5 jit_solution(11399289289626688193)
XLA Ops:
  0.6 4.4 %time_forward.1 = f32[256,24,128]{2,1,0:T(8,128)} custom-call(f32[64,16,256]{2,1,0:T(8,128)} %obs_hbm.1, f32[64,16,256]{2,1,0:T(8,128)} %noise_hbm.1, f32[64,16,256]{2,1,0:T(8,128)} %prior_hbm.1, f32[256,256]{1,0:T(8,128)} %time_ref.1), custom_call_target="tpu_custom_call" | custom-call | flops 805306368 | bytes 6291456 | tf_op jit(solution)/shard_map/time_forward/pallas_call | solution.py:203
  5.1 0.0 copy-start.1
  5.1 0.0 copy-start.2
  5.1 0.0 copy-start.3
  5.1 0.0 copy-start.4
  5.1 0.0 copy-start.5
  5.1 90.8 %all_to_all.10.in_ref = f32[256,24,128]{2,1,0:T(8,128)S(1)} all-to-all(f32[256,24,128]{2,1,0:T(8,128)} %time_forward.1), channel_id=1, replica_groups=mesh['lon'=8,'lat'=32] {'lon','lat'}, dimensions={0} | all-to-all | bytes 6291456 | tf_op jit(solution)/shard_map/all_to_all | solution.py:220
  95.9 0.0 copy-done.1
  95.9 0.0 copy-done.2
  95.9 0.0 copy-done.3
  95.9 0.0 copy-done.4
  95.9 0.0 copy-done.5
  96.0 8.2 %middle.1 = f32[256,16,128]{2,1,0:T(8,128)S(1)} custom-call(f32[256,24,128]{2,1,0:T(8,128)S(1)} %all_to_all.10.in_ref, f32[512,512]{1,0:T(8,128)S(1)} %copy-done.1, f32[512,512]{1,0:T(8,128)S(1)} %copy-done.2, f32[1,512]{1,0:T(1,128)S(1)} %bitcast.4, f32[1,512]{1,0:T(1,128)S(1)} %bitcast.5, f32[256]{0:T(256)S(1)} %copy-done.5), custom_call_target="tpu_custom_call" | custom-call | flops 6442450944 | bytes 8388608 | tf_op jit(solution)/shard_map/middle/pallas_call | solution.py:222
  104.1 0.0 copy-start
  104.2 59.5 %all_to_all.11 = f32[256,16,128]{2,1,0:T(8,128)S(1)} all-to-all(f32[256,16,128]{2,1,0:T(8,128)S(1)} %middle.1), channel_id=1, replica_groups=mesh['lon'=8,'lat'=32] {'lon','lat'}, dimensions={0} | all-to-all | bytes 4194304 | tf_op jit(solution)/shard_map/all_to_all | solution.py:243
  163.6 0.0 copy-done
  163.6 2.9 %time_backward.1 = (f32[64,16,256]{2,1,0:T(8,128)}, f32[64,16,256]{2,1,0:T(8,128)}) custom-call(f32[4096,128]{1,0:T(8,128)S(1)} %bitcast.3, f32[256,256]{1,0:T(8,128)S(1)} %copy-done), custom_call_target="tpu_custom_call" | custom-call | flops 805306368 | bytes 4194304 | tf_op jit(solution)/shard_map/time_backward/pallas_call | solution.py:245
Async XLA Ops:
  5.1 90.8 %copy-start.1 = (f32[512,512]{1,0:T(8,128)S(1)}, f32[512,512]{1,0:T(8,128)}, u32[]{:S(2)}) copy-start(f32[512,512]{1,0:T(8,128)} %lon_ref.1) | copy-start | bytes 3145732
  5.1 90.8 %copy-start.2 = (f32[512,512]{1,0:T(8,128)S(1)}, f32[512,512]{1,0:T(8,128)}, u32[]{:S(2)}) copy-start(f32[512,512]{1,0:T(8,128)} %lat_ref.1) | copy-start | bytes 3145732
  5.1 90.8 %copy-start.3 = (f32[512]{0:T(512)S(1)}, f32[512]{0:T(512)}, u32[]{:S(2)}) copy-start(f32[512]{0:T(512)} %param.15) | copy-start | bytes 6148
  5.1 90.8 %copy-start.4 = (f32[512]{0:T(512)S(1)}, f32[512]{0:T(512)}, u32[]{:S(2)}) copy-start(f32[512]{0:T(512)} %param.16) | copy-start | bytes 6148
  5.1 90.8 %copy-start.5 = (f32[256]{0:T(256)S(1)}, f32[256]{0:T(256)}, u32[]{:S(2)}) copy-start(f32[256]{0:T(256)} %vals_time.1) | copy-start | bytes 3076
  104.1 59.5 %copy-start = (f32[256,256]{1,0:T(8,128)S(1)}, f32[256,256]{1,0:T(8,128)}, u32[]{:S(2)}) copy-start(f32[256,256]{1,0:T(8,128)} %time_ref.1) | copy-start | bytes 786436

commit v6 on v5

--- a/solution.py
+++ b/solution.py
@@ -172,12 +172,11 @@
             left = tuple(half[k_half * 128:(k_half + 1) * 128] for half in basis)
             result = product(left, (field[0], field[1]))
             slots = [f * 4 + j_half * 2 + k_half for f in range(2)]
-            for jj in range(8):
-                block = result[:, jj * 128:(jj + 1) * 128].T
-                for f in range(2):
-                    target = bufs.at[slots[f]].reshape(512, 128)
-                    target[pl.ds(jj, 64, stride=8), :] = block[f * 64:(f + 1) * 64]
+            blocks = [result[:, jj * 128:(jj + 1) * 128].T for jj in range(8)]
             for f, array in enumerate((weights_hbm, sample_hbm)):
+                target = bufs.at[slots[f]].reshape(512, 128)
+                for jj in range(8):
+                    target[pl.ds(jj, 64, stride=8), :] = blocks[jj][f * 64:(f + 1) * 64]
                 copy = pltpu.make_async_copy(
                     bufs.at[slots[f]],
                     array.at[:, pl.ds(j_half * 8, 8), pl.ds(k_half * 128, 128)],

time: 167 us -> 167 us (level)
  no operation moved by 1% of the time
where the time goes in v6:
time: 167 us
  blocking collectives  150 us (90%)
  Pallas kernels  15.6 us (9%)
    all_to_all x1, blocking collectives, on_device(): packed = lax.all_to_all(packed, ('lon', 'lat'), 0, 0, tiled=True)  90.8 us
    all_to_all x1, blocking collectives, on_device(): planes = lax.all_to_all(planes, ('lon', 'lat'), 0, 0, tiled=True)  59.5 us
    pallas_call x1, Pallas kernels, on_device(): pl.pallas_call(middle_kernel, out_shape=shape((256, 16, 128)), in_specs=[...  8.18 us
    pallas_call x1, Pallas kernels, on_device(): pl.pallas_call(forward_kernel, out_shape=shape((256, 24, 128)), in_specs=...  4.44 us

profile of v6, /device:TPU:1, one launch (start us, length us, event | category | flops | bytes accessed | tf_op | source)
XLA Modules:
  0.0 166.6 jit_solution(1847336657626162994)
XLA Ops:
  0.6 4.4 %time_forward.1 = f32[256,24,128]{2,1,0:T(8,128)} custom-call(f32[64,16,256]{2,1,0:T(8,128)} %obs_hbm.1, f32[64,16,256]{2,1,0:T(8,128)} %noise_hbm.1, f32[64,16,256]{2,1,0:T(8,128)} %prior_hbm.1, f32[256,256]{1,0:T(8,128)} %time_ref.1), custom_call_target="tpu_custom_call" | custom-call | flops 805306368 | bytes 6291456 | tf_op jit(solution)/shard_map/time_forward/pallas_call | solution.py:202
  5.1 0.0 copy-start.1
  5.1 0.0 copy-start.2
  5.1 0.0 copy-start.3
  5.1 0.0 copy-start.4
  5.1 0.0 copy-start.5
  5.1 90.8 %all_to_all.10.in_ref = f32[256,24,128]{2,1,0:T(8,128)S(1)} all-to-all(f32[256,24,128]{2,1,0:T(8,128)} %time_forward.1), channel_id=1, replica_groups=mesh['lon'=8,'lat'=32] {'lon','lat'}, dimensions={0} | all-to-all | bytes 6291456 | tf_op jit(solution)/shard_map/all_to_all | solution.py:219
  95.9 0.0 copy-done.1
  95.9 0.0 copy-done.2
  95.9 0.0 copy-done.3
  95.9 0.0 copy-done.4
  95.9 0.0 copy-done.5
  96.0 8.2 %middle.1 = f32[256,16,128]{2,1,0:T(8,128)S(1)} custom-call(f32[256,24,128]{2,1,0:T(8,128)S(1)} %all_to_all.10.in_ref, f32[512,512]{1,0:T(8,128)S(1)} %copy-done.1, f32[512,512]{1,0:T(8,128)S(1)} %copy-done.2, f32[1,512]{1,0:T(1,128)S(1)} %bitcast.4, f32[1,512]{1,0:T(1,128)S(1)} %bitcast.5, f32[256]{0:T(256)S(1)} %copy-done.5), custom_call_target="tpu_custom_call" | custom-call | flops 6442450944 | bytes 8388608 | tf_op jit(solution)/shard_map/middle/pallas_call | solution.py:221
  104.1 0.0 copy-start
  104.2 59.5 %all_to_all.11 = f32[256,16,128]{2,1,0:T(8,128)S(1)} all-to-all(f32[256,16,128]{2,1,0:T(8,128)S(1)} %middle.1), channel_id=1, replica_groups=mesh['lon'=8,'lat'=32] {'lon','lat'}, dimensions={0} | all-to-all | bytes 4194304 | tf_op jit(solution)/shard_map/all_to_all | solution.py:242
  163.6 0.0 copy-done
  163.6 3.0 %time_backward.1 = (f32[64,16,256]{2,1,0:T(8,128)}, f32[64,16,256]{2,1,0:T(8,128)}) custom-call(f32[4096,128]{1,0:T(8,128)S(1)} %bitcast.3, f32[256,256]{1,0:T(8,128)S(1)} %copy-done), custom_call_target="tpu_custom_call" | custom-call | flops 805306368 | bytes 4194304 | tf_op jit(solution)/shard_map/time_backward/pallas_call | solution.py:244
Async XLA Ops:
  5.1 90.8 %copy-start.1 = (f32[512,512]{1,0:T(8,128)S(1)}, f32[512,512]{1,0:T(8,128)}, u32[]{:S(2)}) copy-start(f32[512,512]{1,0:T(8,128)} %lon_ref.1) | copy-start | bytes 3145732
  5.1 90.8 %copy-start.2 = (f32[512,512]{1,0:T(8,128)S(1)}, f32[512,512]{1,0:T(8,128)}, u32[]{:S(2)}) copy-start(f32[512,512]{1,0:T(8,128)} %lat_ref.1) | copy-start | bytes 3145732
  5.1 90.8 %copy-start.3 = (f32[512]{0:T(512)S(1)}, f32[512]{0:T(512)}, u32[]{:S(2)}) copy-start(f32[512]{0:T(512)} %param.15) | copy-start | bytes 6148
  5.1 90.8 %copy-start.4 = (f32[512]{0:T(512)S(1)}, f32[512]{0:T(512)}, u32[]{:S(2)}) copy-start(f32[512]{0:T(512)} %param.16) | copy-start | bytes 6148
  5.1 90.8 %copy-start.5 = (f32[256]{0:T(256)S(1)}, f32[256]{0:T(256)}, u32[]{:S(2)}) copy-start(f32[256]{0:T(256)} %vals_time.1) | copy-start | bytes 3076
  104.1 59.5 %copy-start = (f32[256,256]{1,0:T(8,128)S(1)}, f32[256,256]{1,0:T(8,128)}, u32[]{:S(2)}) copy-start(f32[256,256]{1,0:T(8,128)} %time_ref.1) | copy-start | bytes 786436
